TPU v7x, 256 devices: a whole 4x4x8 slice. The times are simulated.
256 devices in a mesh: grp: 8 (over x, core), dev: 32 (over y, z).
Axes of the slice: x: 4, y: 4, z: 8, core: 2. Of those that a mesh axis runs over, the one named last changes fastest.
Arguments:
- table: bfloat16 [16384, 1024], P('dev'), may hold values from -6 to 6
- target_table: bfloat16 [16384, 256], P('dev'), may hold values from -6 to 6
- centres: bfloat16 [131072, 1024], P(('grp', 'dev')), may hold values from -6 to 6
- coefficients: float32 [131072, 256], P(('grp', 'dev')), may hold values from -6 to 6
- batch_index: int32 [2, 256], replicated, may hold values from 0 to 16383
Outputs:
- coefficients_out: float32 [131072, 256], P(('grp', 'dev'))
- residuals: float32 [2, 256, 256], replicated
Inputs may be any that keep to these rules, and one draw needn't show every extreme that they name: `batch_index`: row numbers into the descriptor table.
All inputs are finite; a program needn't handle non-finite values.
Results may differ from a plain program's by a relative error of at most 0.0004.
Values may be sent and summed in bfloat16 or wider, within the bound.
A program may use at most 64 MiB of HBM per device.

v0:
```python
import math

import jax
import jax.numpy as jnp
from jax import lax
from jax.sharding import PartitionSpec as P

STEPS = 2


SPREAD = 2.0
RATE = 2.0


def in_blocks(array, dim, length):
    before, after = (array.shape[:dim], array.shape[dim + 1 :])
    return jnp.moveaxis(array.reshape(*before, length, -1, *after), dim, 0)


def sum_at_owner(array, axis, dim):
    length = lax.axis_size(axis)
    parts = lax.all_to_all(in_blocks(array, dim, length), axis, 0, 0, tiled=True)
    return jnp.sum(parts.astype(jnp.float32), axis=0)


def filled_up(lines, length):
    spare = -lines.shape[0] % length
    if not spare:
        return lines
    return jnp.concatenate([lines, jnp.zeros((spare, *lines.shape[1:]), lines.dtype)])


def from_everyone(array, axis):
    copies = jnp.broadcast_to(array, (lax.axis_size(axis), *array.shape))
    return lax.all_to_all(copies, axis, split_axis=0, concat_axis=0, tiled=True)


def in_order(parts, dim):
    lengths = list(parts.shape[1:])
    lengths[dim] *= parts.shape[0]
    return jnp.moveaxis(parts, 0, dim).reshape(lengths)


def collect(array, axis, dim):
    parts = from_everyone(array, axis)
    return in_order(parts, dim)


def nested_sum(array, axes):
    lines = array.reshape(-1, array.shape[-1])
    own = sum_at_owner(filled_up(lines, lax.axis_size(axes)), axes, 0)
    whole = collect(own.astype(jnp.bfloat16), axes, 0)
    return whole[: len(lines)].reshape(array.shape).astype(jnp.float32)


def sent_and_summed(array, axis, dim):
    parts = in_blocks(array, dim, lax.axis_size(axis))
    arrived = lax.all_to_all(parts, axis, split_axis=0, concat_axis=0, tiled=True)
    return arrived.sum(axis=0)


def in_one_piece(arrays, axis, dim, along):
    widths = [math.prod(a.shape[along:]) for a in arrays]
    both = jnp.concatenate(
        [a.reshape(*a.shape[:along], w) for a, w in zip(arrays, widths)], axis=along
    )
    whole = sent_and_summed(both, axis, dim)
    parts = jnp.split(whole, [sum(widths[:k]) for k in range(1, len(widths))], axis=along)
    return tuple((b.reshape(*whole.shape[:along], *a.shape[along:]) for a, b in zip(arrays, parts)))


def over_copies(array, axis):
    return from_everyone(array, axis).sum(axis=0)


def in_one(arrays, axis):
    ends = [0]
    for a in arrays:
        ends.append(ends[-1] + a.size)
    total = over_copies(jnp.concatenate([a.ravel() for a in arrays]), axis)
    return tuple((total[b:e].reshape(a.shape) for a, b, e in zip(arrays, ends, ends[1:])))


def in_one_piece_2(arrays, axis, dim, along):
    widths = [math.prod(a.shape[along:]) for a in arrays]
    both = jnp.concatenate(
        [a.reshape(*a.shape[:along], w) for a, w in zip(arrays, widths)], axis=along
    )
    whole = lax.all_gather(both, axis, axis=dim, tiled=True)
    parts = jnp.split(whole, [sum(widths[:k]) for k in range(1, len(widths))], axis=along)
    return tuple((b.reshape(*whole.shape[:along], *a.shape[along:]) for a, b in zip(arrays, parts)))


def laplace(rows, centres, centre_norm, radius):
    row_norm = jnp.sum(jnp.square(rows.astype(jnp.float32)), axis=1)
    cross = lax.dot_general(
        rows, centres, (((1,), (1,)), ((), ())), preferred_element_type=jnp.float32
    )
    squared = row_norm[:, None] + centre_norm[None, :] - 2.0 * cross
    dist = jnp.sqrt(jnp.maximum(squared, 0.0))
    return jnp.exp((radius - dist) / SPREAD)


def body(table, target_table, centres, coefficients, batch_index):
    groups = lax.axis_size("grp")
    members = lax.axis_size("dev")
    tab_rows = table.shape[0]
    batch = batch_index.shape[1]
    total = centres.shape[0] * groups * members
    scale = 1.0 / math.sqrt(total)
    radius = math.sqrt(2.0 * centres.shape[1])
    owner = lax.axis_index("dev") * tab_rows
    local = batch_index.reshape(-1) - owner
    inside = ((local >= 0) & (local < tab_rows)).astype(jnp.bfloat16)[:, None]
    safe = jnp.clip(local, 0, tab_rows - 1)
    pick_rows = jnp.take(table, safe, axis=0) * inside
    pick_aims = jnp.take(target_table, safe, axis=0) * inside
    every_rows = pick_rows
    every_aims = pick_aims
    every_rows, every_aims = (nested_sum(every_rows, "dev"), nested_sum(every_aims, "dev"))
    every_rows = every_rows.astype(jnp.bfloat16)
    centre_norm = jnp.sum(jnp.square(centres.astype(jnp.float32)), axis=1)
    coef = coefficients
    kept = []
    for step in range(STEPS):
        rows = every_rows[step * batch : (step + 1) * batch]
        aims = every_aims[step * batch : (step + 1) * batch]
        weights = laplace(rows, centres, centre_norm, radius)
        partial_value = (
            jnp.dot(
                weights, coef, precision=lax.Precision.HIGHEST, preferred_element_type=jnp.float32
            )
            * scale
        )
        mass_part = jnp.sum(weights, axis=1) * scale
        share, mass_share = in_one_piece((partial_value, mass_part), "dev", 0, 1)
        share, mass_share = in_one((share, mass_share), "grp")
        width = share.shape[0]
        aim_share = lax.dynamic_slice_in_dim(aims, lax.axis_index("dev") * width, width, 0)
        resid, mass = in_one_piece_2((share - aim_share, mass_share), "dev", 0, 1)
        along = jnp.dot(mass, resid, precision=lax.Precision.HIGHEST) / jnp.sum(mass * mass)
        proj = resid - mass[:, None] * along[None, :]
        grad = lax.dot_general(
            weights,
            proj,
            (((0,), (0,)), ((), ())),
            precision=lax.Precision.HIGHEST,
            preferred_element_type=jnp.float32,
        )
        coef = coef - grad * (RATE * scale)
        kept.append(resid)
    return (coef, jnp.stack(kept))


def solution(mesh):
    in_specs = (
        P("dev", None),
        P("dev", None),
        P(("grp", "dev"), None),
        P(("grp", "dev"), None),
        P(),
    )
    out_specs = (P(("grp", "dev"), None), P())
    return jax.shard_map(body, mesh=mesh, in_specs=in_specs, out_specs=out_specs, check_vma=False)
```

profile of v0, /device:TPU:2, one launch (start us, length us, event | category | flops | bytes accessed | tf_op | source)
XLA Modules:
  0.0 274.6 jit_solution(8957341785297864945)
XLA Ops:
  3.0 2.1 gather_fusion
  5.1 1.2 select_multiply_fusion
  6.3 11.6 %all-to-all-start = ((bf16[32,16,1024]{2,1,0:T(8,128)(2,1)}), bf16[32,16,1024]{2,1,0:T(8,128)(2,1)S(1)}, u32[]{:S(2)}, u32[]{:S(2)}) async-start(bf16[32,16,1024]{2,1,0:T(8,128)(2,1)} %select_multiply_fusion), calls=%async_computation | async-start | bytes 2097152 | tf_op jit(solution)/shard_map/all_to_all | solution.py:22
  17.9 2.0 gather_fusion.1
  20.8 25.8 %all-to-all-done = bf16[32,16,1024]{2,1,0:T(8,128)(2,1)S(1)} async-done(((bf16[32,16,1024]{2,1,0:T(8,128)(2,1)}), bf16[32,16,1024]{2,1,0:T(8,128)(2,1)S(1)}, u32[]{:S(2)}, u32[]{:S(2)}) %all-to-all-start) | async-done | bytes 1048608 | tf_op jit(solution)/shard_map/all_to_all | solution.py:22
  46.5 5.1 %all-to-all-start.4 = ((bf16[32,16,256]{2,1,0:T(8,128)(2,1)}), bf16[32,16,256]{2,1,0:T(8,128)(2,1)S(1)}, u32[]{:S(2)}, u32[]{:S(2)}) async-start(bf16[32,16,256]{2,1,0:T(8,128)(2,1)} %select_multiply_fusion.1), calls=%async_computation.4 | async-start | bytes 524288 | tf_op jit(solution)/shard_map/all_to_all | solution.py:22
  51.8 11.6 %all-to-all-done.4 = bf16[32,16,256]{2,1,0:T(8,128)(2,1)S(1)} async-done(((bf16[32,16,256]{2,1,0:T(8,128)(2,1)}), bf16[32,16,256]{2,1,0:T(8,128)(2,1)S(1)}, u32[]{:S(2)}, u32[]{:S(2)}) %all-to-all-start.4) | async-done | bytes 262176 | tf_op jit(solution)/shard_map/all_to_all | solution.py:22
  63.4 1.1 broadcast_in_dim.41
  64.5 4.7 %all-to-all-start.1 = ((bf16[32,16,1024]{2,1,0:T(8,128)(2,1)}), bf16[32,16,1024]{2,1,0:T(8,128)(2,1)S(1)}, u32[]{:S(2)}, u32[]{:S(2)}) async-start(bf16[32,16,1024]{2,1,0:T(8,128)(2,1)} %broadcast_in_dim.41), calls=%async_computation.1 | async-start | bytes 2097152 | tf_op jit(solution)/shard_map/all_to_all | solution.py:35
  70.2 26.7 %all-to-all-done.1 = bf16[32,16,1024]{2,1,0:T(8,128)(2,1)S(1)} async-done(((bf16[32,16,1024]{2,1,0:T(8,128)(2,1)}), bf16[32,16,1024]{2,1,0:T(8,128)(2,1)S(1)}, u32[]{:S(2)}, u32[]{:S(2)}) %all-to-all-start.1) | async-done | bytes 1048608 | tf_op jit(solution)/shard_map/all_to_all | solution.py:35
  97.7 4.9 %all-to-all-start.5 = ((bf16[32,16,256]{2,1,0:T(8,128)(2,1)}), bf16[32,16,256]{2,1,0:T(8,128)(2,1)S(1)}, u32[]{:S(2)}, u32[]{:S(2)}) async-start(bf16[32,16,256]{2,1,0:T(8,128)(2,1)} %broadcast_in_dim.45), calls=%async_computation.5 | async-start | bytes 524288 | tf_op jit(solution)/shard_map/all_to_all | solution.py:35
  103.1 1.1 copy-done.4
  106.6 7.3 %all-to-all-done.5 = bf16[32,16,256]{2,1,0:T(8,128)(2,1)S(1)} async-done(((bf16[32,16,256]{2,1,0:T(8,128)(2,1)}), bf16[32,16,256]{2,1,0:T(8,128)(2,1)S(1)}, u32[]{:S(2)}, u32[]{:S(2)}) %all-to-all-start.5) | async-done | bytes 262176 | tf_op jit(solution)/shard_map/all_to_all | solution.py:35
  113.9 4.5 %all-to-all-start.2 = ((f32[32,8,257]{2,1,0:T(8,128)}), f32[32,8,257]{2,1,0:T(8,128)S(1)}, u32[]{:S(2)}, u32[]{:S(2)}) async-start(f32[32,8,257]{2,1,0:T(8,128)} %pad_maximum_fusion.1), calls=%async_computation.2 | async-start | bytes 786432 | tf_op jit(solution)/shard_map/all_to_all | solution.py:58
  119.3 2.0 fusion.33
  121.3 9.9 %all-to-all-done.2 = f32[32,8,257]{2,1,0:T(8,128)S(1)} async-done(((f32[32,8,257]{2,1,0:T(8,128)}), f32[32,8,257]{2,1,0:T(8,128)S(1)}, u32[]{:S(2)}, u32[]{:S(2)}) %all-to-all-start.2) | async-done | bytes 263200 | tf_op jit(solution)/shard_map/all_to_all | solution.py:58
  132.1 4.8 %all-to-all-start.3 = ((f32[8,1,2056]{2,1,0:T(1,128)}), f32[8,1,2056]{2,1,0:T(1,128)S(1)}, u32[]{:S(2)}, u32[]{:S(2)}) async-start(f32[8,1,2056]{2,1,0:T(1,128)} %broadcast_in_dim.42), calls=%async_computation.3 | async-start | bytes 139264 | tf_op jit(solution)/shard_map/all_to_all | solution.py:35
  137.8 3.3 %all-to-all-done.3 = f32[8,1,2056]{2,1,0:T(1,128)S(1)} async-done(((f32[8,1,2056]{2,1,0:T(1,128)}), f32[8,1,2056]{2,1,0:T(1,128)S(1)}, u32[]{:S(2)}, u32[]{:S(2)}) %all-to-all-start.3) | async-done | bytes 65824 | tf_op jit(solution)/shard_map/all_to_all | solution.py:35
  142.0 48.3 %all_gather.6 = f32[256,257]{1,0:T(8,128)S(1)} all-gather(f32[8,257]{1,0:T(8,128)S(1)} %pad_maximum_fusion.4), channel_id=1, replica_groups=mesh['grp'=8,'dev'=32] {'dev'}, dimensions={0}, use_global_device_ids=true | all-gather | bytes 271392 | tf_op jit(solution)/shard_map/all_gather | solution.py:89
  194.0 16.7 %all_to_all.42 = f32[32,8,257]{2,1,0:T(8,128)S(1)} all-to-all(f32[32,8,257]{2,1,0:T(8,128)S(1)} %pad_maximum_fusion.2), channel_id=1, replica_groups=mesh['grp'=8,'dev'=32] {'dev'}, dimensions={0} | all-to-all | bytes 526336 | tf_op jit(solution)/shard_map/all_to_all | solution.py:58
  211.5 4.7 %all-to-all-start.7 = ((f32[8,1,2056]{2,1,0:T(1,128)}), f32[8,1,2056]{2,1,0:T(1,128)S(1)}, u32[]{:S(2)}, u32[]{:S(2)}) async-start(f32[8,1,2056]{2,1,0:T(1,128)} %broadcast_in_dim.46), calls=%async_computation.7 | async-start | bytes 139264 | tf_op jit(solution)/shard_map/all_to_all | solution.py:35
  216.3 4.2 %all-to-all-done.7 = f32[8,1,2056]{2,1,0:T(1,128)S(1)} async-done(((f32[8,1,2056]{2,1,0:T(1,128)}), f32[8,1,2056]{2,1,0:T(1,128)S(1)}, u32[]{:S(2)}, u32[]{:S(2)}) %all-to-all-start.7) | async-done | bytes 65824 | tf_op jit(solution)/shard_map/all_to_all | solution.py:35
  221.4 48.9 %all_gather.7 = f32[256,257]{1,0:T(8,128)S(1)} all-gather(f32[8,257]{1,0:T(8,128)S(1)} %pad_maximum_fusion.6), channel_id=1, replica_groups=mesh['grp'=8,'dev'=32] {'dev'}, dimensions={0}, use_global_device_ids=true | all-gather | bytes 271392 | tf_op jit(solution)/shard_map/all_gather | solution.py:89
  271.9 1.9 fusion.12
  (81 shorter events, 19.3 us)
Async XLA Ops:
  0.6 2.4 copy-start
  6.3 11.6 %copy-start.1 = (bf16[512,256]{1,0:T(8,128)(2,1)S(1)}, bf16[512,256]{1,0:T(8,128)(2,1)}, u32[]{:S(2)}) copy-start(bf16[512,256]{1,0:T(8,128)(2,1)} %param.6) | copy-start | bytes 786436
  6.3 40.3 %all-to-all-start = ((bf16[32,16,1024]{2,1,0:T(8,128)(2,1)}), bf16[32,16,1024]{2,1,0:T(8,128)(2,1)S(1)}, u32[]{:S(2)}, u32[]{:S(2)}) async-start(bf16[32,16,1024]{2,1,0:T(8,128)(2,1)} %select_multiply_fusion), calls=%async_computation | async-start | bytes 2097152 | tf_op jit(solution)/shard_map/all_to_all | solution.py:22
  46.5 16.9 %all-to-all-start.4 = ((bf16[32,16,256]{2,1,0:T(8,128)(2,1)}), bf16[32,16,256]{2,1,0:T(8,128)(2,1)S(1)}, u32[]{:S(2)}, u32[]{:S(2)}) async-start(bf16[32,16,256]{2,1,0:T(8,128)(2,1)} %select_multiply_fusion.1), calls=%async_computation.4 | async-start | bytes 524288 | tf_op jit(solution)/shard_map/all_to_all | solution.py:22
  63.4 1.1 copy-start.5
  64.5 4.7 %copy-start.3 = (bf16[512,1024]{1,0:T(8,128)(2,1)S(1)}, bf16[512,1024]{1,0:T(8,128)(2,1)}, u32[]{:S(2)}) copy-start(bf16[512,1024]{1,0:T(8,128)(2,1)} %param.7) | copy-start | bytes 3145732
  64.5 32.4 %all-to-all-start.1 = ((bf16[32,16,1024]{2,1,0:T(8,128)(2,1)}), bf16[32,16,1024]{2,1,0:T(8,128)(2,1)S(1)}, u32[]{:S(2)}, u32[]{:S(2)}) async-start(bf16[32,16,1024]{2,1,0:T(8,128)(2,1)} %broadcast_in_dim.41), calls=%async_computation.1 | async-start | bytes 2097152 | tf_op jit(solution)/shard_map/all_to_all | solution.py:35
  69.2 1.0 copy-start.6
  97.7 16.2 %all-to-all-start.5 = ((bf16[32,16,256]{2,1,0:T(8,128)(2,1)}), bf16[32,16,256]{2,1,0:T(8,128)(2,1)S(1)}, u32[]{:S(2)}, u32[]{:S(2)}) async-start(bf16[32,16,256]{2,1,0:T(8,128)(2,1)} %broadcast_in_dim.45), calls=%async_computation.5 | async-start | bytes 524288 | tf_op jit(solution)/shard_map/all_to_all | solution.py:35
  103.0 1.2 copy-start.4
  104.2 1.0 copy-start.2
  113.9 17.3 %all-to-all-start.2 = ((f32[32,8,257]{2,1,0:T(8,128)}), f32[32,8,257]{2,1,0:T(8,128)S(1)}, u32[]{:S(2)}, u32[]{:S(2)}) async-start(f32[32,8,257]{2,1,0:T(8,128)} %pad_maximum_fusion.1), calls=%async_computation.2 | async-start | bytes 786432 | tf_op jit(solution)/shard_map/all_to_all | solution.py:58
  132.1 9.0 %all-to-all-start.3 = ((f32[8,1,2056]{2,1,0:T(1,128)}), f32[8,1,2056]{2,1,0:T(1,128)S(1)}, u32[]{:S(2)}, u32[]{:S(2)}) async-start(f32[8,1,2056]{2,1,0:T(1,128)} %broadcast_in_dim.42), calls=%async_computation.3 | async-start | bytes 139264 | tf_op jit(solution)/shard_map/all_to_all | solution.py:35
  193.0 0.9 copy-start.7
  211.5 8.9 %all-to-all-start.7 = ((f32[8,1,2056]{2,1,0:T(1,128)}), f32[8,1,2056]{2,1,0:T(1,128)S(1)}, u32[]{:S(2)}, u32[]{:S(2)}) async-start(f32[8,1,2056]{2,1,0:T(1,128)} %broadcast_in_dim.46), calls=%async_computation.7 | async-start | bytes 139264 | tf_op jit(solution)/shard_map/all_to_all | solution.py:35
where the time goes:
time: 276 us; the launch traced here: 275 us
  blocking collectives  114 us (41%)
  waiting for transfers between devices  88.8 us (32%)
  starting transfers between devices  40.4 us (15%)
  local copies, waits for them, and re-layouts  12.3 us (4%)
  other arithmetic  11.1 us (4%)
  matrix products  7.24 us (3%)
    all_gather x2, blocking collectives, in_one_piece_2(): whole = lax.all_gather(both, axis, axis=dim, tiled=True)  97.2 us
    all_to_all x4, waiting for transfers between devices, from_everyone(): return lax.all_to_all(copies, axis, split_axis=0, concat_axis=0, tiled=True)  41.5 us
    all_to_all x2, waiting for transfers between devices, sum_at_owner(): lax.all_to_all(in_blocks(array, dim, length), axis, 0, 0, tiled=True)  37.4 us
    all_to_all x4, starting transfers between devices, from_everyone(): return lax.all_to_all(copies, axis, split_axis=0, concat_axis=0, tiled=True)  19.2 us
    all_to_all x1, blocking collectives, sent_and_summed(): lax.all_to_all(parts, axis, split_axis=0, concat_axis=0, tiled=True)  16.7 us
    all_to_all x2, starting transfers between devices, sum_at_owner(): lax.all_to_all(in_blocks(array, dim, length), axis, 0, 0, tiled=True)  16.7 us
    all_to_all x1, waiting for transfers between devices, sent_and_summed(): lax.all_to_all(parts, axis, split_axis=0, concat_axis=0, tiled=True)  9.91 us
  transfers between devices with their start and end apart: 7, of which 7 were waited for; matrix products, arithmetic and copies ran while one was open for 4% of the time, Pallas kernels for 0%

commit v1 on v0

v1 whole, which is shorter than its diff:
```python
import math

import jax
import jax.numpy as jnp
from jax import lax
from jax.experimental import pallas as pl
from jax.experimental.pallas import tpu as pltpu
from jax.sharding import PartitionSpec as P

MESH = pl.DeviceIdType.MESH
SPREAD = 2.0
RATE = 2.0
NX, NC, NY, NZ = 4, 2, 4, 8
NP = NX * NY
ND = NY * NZ
F32 = jnp.float32
BF16 = jnp.bfloat16
HI = lax.Precision.HIGHEST
NT = (((1,), (1,)), ((), ()))
TN = (((0,), (0,)), ((), ()))
Z_ORDER = (4, 3, 5, 2, 6, 1, 7)


def dot(a, b, dims=(((1,), (0,)), ((), ())), precision=None):
    return lax.dot_general(a, b, dims, precision=precision, preferred_element_type=F32)


def kernel(
    table, target, centres, coef, index,
    coef_out, resid_out,
    tab_v, tgt_v, cen_v, cf_v, idx_v, aims_v,
    pick, parts, rows,
    w_v, core_send, core_recv, xy_send, xy_recv, z_buf, whole,
    load_sem, a_send, a_recv, az_recv, axy_recv, ac_recv,
    cc_send, cc_recv, cxy_recv, cz_recv, gxy_recv, gc_recv,
):
    g = lax.axis_index("grp")
    d = lax.axis_index("dev")
    x, c = g // 2, g % 2
    y, z = d // NZ, d % NZ
    p = x * NY + y
    feat = c * NX + x
    chunk = z * NY + y
    radius = math.sqrt(2.0 * 1024)
    scale = 1.0 / math.sqrt(131072)

    def at_dev(k):
        return {"grp": g, "dev": k}

    def at_xy(k):
        q = lax.rem(p + k, NP)
        return q, {"grp": (q // NY) * 2 + c, "dev": (q % NY) * NZ + z}

    sibling = {"grp": x * 2 + 1 - c, "dev": d}

    barrier = pltpu.get_barrier_semaphore()

    def greet_dev(k, _):
        pl.semaphore_signal(barrier, inc=1, device_id=at_dev(lax.rem(d + k, ND)), device_id_type=MESH)
        return 0

    def greet_x(k, _):
        dx, ty = 1 + k // NY, k % NY
        tx = lax.rem(x + dx, NX)
        pl.semaphore_signal(
            barrier, inc=1, device_id={"grp": tx * 2 + c, "dev": ty * NZ + z}, device_id_type=MESH
        )
        return 0

    lax.fori_loop(1, ND, greet_dev, 0)
    lax.fori_loop(0, (NX - 1) * NY, greet_x, 0)
    pl.semaphore_signal(barrier, inc=1, device_id=sibling, device_id_type=MESH)

    loads = [
        pltpu.make_async_copy(index, idx_v, load_sem.at[0]),
        pltpu.make_async_copy(
            table.at[:, pl.ds(pl.multiple_of(feat * 128, 128), 128)], tab_v, load_sem.at[1]
        ),
        pltpu.make_async_copy(target, tgt_v, load_sem.at[2]),
        pltpu.make_async_copy(centres, cen_v, load_sem.at[3]),
        pltpu.make_async_copy(coef, cf_v, load_sem.at[4]),
    ]
    for load in loads:
        load.start()

    loads[0].wait()
    here = lax.broadcasted_iota(jnp.int32, (512, 256), 0) + d * 512
    hot = jnp.concatenate(
        [(here == idx_v[s : s + 1, :]).astype(F32).astype(BF16) for s in range(2)], axis=1
    )
    loads[1].wait()
    pick[...] = dot(hot, tab_v[...], TN).astype(BF16).reshape(ND, 16, 128)
    parts[chunk] = pick[chunk]

    pl.semaphore_wait(barrier, ND - 1 + (NX - 1) * NY + 1)

    def send_pick(k, _):
        to = lax.rem(d + k, ND)
        slot = (to % NZ) * NY + to // NZ
        pltpu.make_async_remote_copy(
            src_ref=pick.at[slot], dst_ref=parts.at[chunk], send_sem=a_send.at[0], recv_sem=a_recv,
            device_id=at_dev(to), device_id_type=MESH,
        ).start()
        return 0

    lax.fori_loop(1, ND, send_pick, 0)

    loads[2].wait()
    first = (g == 0).astype(F32)
    aims_v[...] = dot(hot, tgt_v[...], TN) * first
    loads[3].wait()
    square = jnp.square(cen_v[...].astype(F32))
    high = square.astype(BF16)
    low = (square - high.astype(F32)).astype(BF16)
    ones = jnp.ones((8, 1024), BF16)
    cnorm = (dot(ones, high, NT) + dot(ones, low, NT))[0:1, :]

    def wait_bytes(ref, sem):
        pltpu.make_async_copy(ref, ref, sem).wait()

    wait_bytes(parts.at[pl.ds(0, ND - 1)], a_recv)
    own = jnp.sum(parts[...].astype(F32), axis=0).astype(BF16)
    lane = pl.ds(pl.multiple_of(feat * 128, 128), 128)
    rows[pl.ds(pl.multiple_of(chunk * 16, 16), 16), lane] = own

    def block(zz):
        return rows.at[pl.ds(pl.multiple_of((zz * NY + y) * 16, 16), 16), lane]

    for k in Z_ORDER:
        pltpu.make_async_remote_copy(
            src_ref=block(z), dst_ref=block(z), send_sem=a_send.at[1], recv_sem=az_recv.at[k],
            device_id=at_dev(y * NZ + lax.rem(z + k, NZ)), device_id_type=MESH,
        ).start()

    def pass_on(k):
        zz = lax.rem(z + NZ - k, NZ)

        def one(j, _):
            _, to = at_xy(j)
            pltpu.make_async_remote_copy(
                src_ref=block(zz), dst_ref=block(zz), send_sem=a_send.at[2], recv_sem=axy_recv.at[k],
                device_id=to, device_id_type=MESH,
            ).start()
            return 0

        lax.fori_loop(1, NP, one, 0)

    pass_on(0)
    for k in (1, 7, 2, 6, 3, 5, 4):
        wait_bytes(block(z), az_recv.at[k])
        pass_on(k)

    half = pl.ds(pl.multiple_of(c * 512, 512), 512)
    to_core = []
    for k in (0, 1, 7, 2, 6, 3, 5, 4):
        zz = lax.rem(z + NZ - k, NZ)
        wait_bytes(parts.at[pl.ds(0, NP - 1)], axy_recv.at[k])
        strip = rows.at[pl.ds(pl.multiple_of(zz * 64, 64), 64), half]
        copy = pltpu.make_async_remote_copy(
            src_ref=strip, dst_ref=strip, send_sem=a_send.at[3], recv_sem=ac_recv,
            device_id=sibling, device_id_type=MESH,
        )
        copy.start()
    wait_bytes(rows.at[:, pl.ds(0, 512)], ac_recv)

    all_rows = rows[...]
    rnorm = jnp.sum(jnp.square(all_rows.astype(F32)), axis=1, keepdims=True)
    cross = dot(all_rows, cen_v[...], NT)
    dist = jnp.sqrt(jnp.maximum(rnorm + cnorm - 2.0 * cross, 0.0))
    w_v[...] = jnp.exp((radius - dist) / SPREAD) * scale
    loads[4].wait()

    mass0 = dot(jnp.ones((8, 512), F32), w_v[0:256, :], NT, HI)
    mass1 = dot(jnp.ones((8, 512), F32), w_v[256:512, :], NT, HI)
    mass = jnp.concatenate(
        [mass0[0:1, 0:128], mass0[0:1, 128:256], mass1[0:1, 0:128], mass1[0:1, 128:256],
         jnp.zeros((4, 128), F32)], axis=0,
    )

    def partials(h, dst):
        r0 = pl.ds(pl.multiple_of(h * 128, 128), 128)
        r1 = pl.ds(pl.multiple_of(h * 128 + 256, 128), 128)
        w0, w1 = w_v[r0, :], w_v[r1, :]
        s0 = dot(w0, cf_v[...], precision=HI) - aims_v[r0, :]
        s1 = dot(w1, cf_v[...], precision=HI) - aims_v[r1, :]
        gram = dot(w1, w_v[0:256, :], NT, HI)
        for n, part in enumerate((s0, s1, gram)):
            for m in range(2):
                at = n * 16 + m * 8
                dst[:, at : at + 8, :] = part[:, m * 128 : m * 128 + 128].reshape(NP, 8, 128)
        dst[:, 48:56, :] = jnp.broadcast_to(mass[None], (NP, 8, 128))

    partials(1 - c, core_send)
    core_copy = pltpu.make_async_remote_copy(
        src_ref=core_send, dst_ref=core_recv, send_sem=cc_send, recv_sem=cc_recv,
        device_id=sibling, device_id_type=MESH,
    )
    core_copy.start()
    partials(c, xy_send)
    core_copy.wait()
    xy_send[...] = xy_send[...] + core_recv[...]
    xy_recv[p] = xy_send[p]

    def send_sum(k, _):
        q, to = at_xy(k)
        pltpu.make_async_remote_copy(
            src_ref=xy_send.at[q], dst_ref=xy_recv.at[p], send_sem=a_send.at[4], recv_sem=cxy_recv,
            device_id=to, device_id_type=MESH,
        ).start()
        return 0

    lax.fori_loop(1, NP, send_sum, 0)
    wait_bytes(xy_recv.at[pl.ds(0, NP - 1)], cxy_recv)
    z_buf[z] = jnp.sum(xy_recv[...], axis=0)

    for k in Z_ORDER:
        pltpu.make_async_remote_copy(
            src_ref=z_buf.at[z], dst_ref=z_buf.at[z], send_sem=a_send.at[5], recv_sem=cz_recv,
            device_id=at_dev(y * NZ + lax.rem(z + k, NZ)), device_id_type=MESH,
        ).start()
    wait_bytes(z_buf.at[pl.ds(0, NZ - 1)], cz_recv)
    total = jnp.sum(z_buf[...], axis=0)
    whole[c, p] = total[0:48]

    def send_whole(k, _):
        _, to = at_xy(k)
        pltpu.make_async_remote_copy(
            src_ref=whole.at[c, p], dst_ref=whole.at[c, p], send_sem=a_send.at[6], recv_sem=gxy_recv,
            device_id=to, device_id_type=MESH,
        ).start()
        return 0

    lax.fori_loop(1, NP, send_whole, 0)
    wait_bytes(whole.at[0, pl.ds(0, NP - 1)], gxy_recv)
    last = pltpu.make_async_remote_copy(
        src_ref=whole.at[c], dst_ref=whole.at[c], send_sem=a_send.at[7], recv_sem=gc_recv,
        device_id=sibling, device_id_type=MESH,
    )
    last.start()
    last.wait()

    def piece(n):
        halves = [
            jnp.concatenate(
                [whole[h, :, n * 16 + m * 8 : n * 16 + m * 8 + 8, :].reshape(128, 128) for m in range(2)],
                axis=1,
            )
            for h in range(2)
        ]
        return jnp.concatenate(halves, axis=0)

    def project(resid, m):
        row = jnp.concatenate([total[48 + 2 * m : 49 + 2 * m], total[49 + 2 * m : 50 + 2 * m]], axis=1)
        row8 = jnp.broadcast_to(row, (8, 256))
        along = dot(row8, resid, precision=HI) / jnp.sum(row * row)
        only = (lax.broadcasted_iota(jnp.int32, (8, 256), 0) == 0).astype(F32)
        return resid - dot(row8 * only, along, TN, HI)

    resid0 = piece(0)
    resid_out[0] = resid0
    proj0 = project(resid0, 0)
    resid1 = piece(1) - RATE * dot(piece(2), proj0, precision=HI)
    resid_out[1] = resid1
    proj1 = project(resid1, 1)
    grad = dot(w_v[...], jnp.concatenate([proj0, proj1], axis=0), TN, HI)
    coef_out[...] = cf_v[...] - RATE * grad

    wait_bytes(parts.at[pl.ds(0, ND - 1)], a_send.at[0])
    wait_bytes(parts.at[pl.ds(0, NZ - 1)], a_send.at[1])
    for _ in range(1):
        wait_bytes(rows.at[pl.ds(0, 480), pl.ds(0, 512)], a_send.at[2])
    wait_bytes(rows.at[:, pl.ds(0, 512)], a_send.at[3])
    wait_bytes(xy_recv.at[pl.ds(0, NP - 1)], a_send.at[4])
    wait_bytes(z_buf.at[pl.ds(0, NZ - 1)], a_send.at[5])
    wait_bytes(whole.at[0, pl.ds(0, NP - 1)], a_send.at[6])


def body(table, target_table, centres, coefficients, batch_index):
    dma = pltpu.SemaphoreType.DMA
    return pl.pallas_call(
        kernel,
        name="regression_steps",
        out_shape=(
            jax.ShapeDtypeStruct((512, 256), F32),
            jax.ShapeDtypeStruct((2, 256, 256), F32),
        ),
        in_specs=[pl.BlockSpec(memory_space=pl.ANY)] * 5,
        out_specs=(pl.BlockSpec(memory_space=pltpu.VMEM), pl.BlockSpec(memory_space=pltpu.VMEM)),
        scratch_shapes=[
            pltpu.VMEM((512, 128), BF16),
            pltpu.VMEM((512, 256), BF16),
            pltpu.VMEM((512, 1024), BF16),
            pltpu.VMEM((512, 256), F32),
            pltpu.VMEM((2, 256), jnp.int32),
            pltpu.VMEM((512, 256), F32),
            pltpu.VMEM((ND, 16, 128), BF16),
            pltpu.VMEM((ND, 16, 128), BF16),
            pltpu.VMEM((512, 1024), BF16),
            pltpu.VMEM((512, 512), F32),
            pltpu.VMEM((NP, 56, 128), F32),
            pltpu.VMEM((NP, 56, 128), F32),
            pltpu.VMEM((NP, 56, 128), F32),
            pltpu.VMEM((NP, 56, 128), F32),
            pltpu.VMEM((NZ, 56, 128), F32),
            pltpu.VMEM((2, NP, 48, 128), F32),
            dma((5,)), dma((8,)), dma, dma((NZ,)), dma((NZ,)), dma,
            dma, dma, dma, dma, dma, dma,
        ],
        compiler_params=pltpu.CompilerParams(
            collective_id=0, has_side_effects=True, vmem_limit_bytes=56 * 2**20
        ),
    )(table, target_table, centres, coefficients, batch_index)


def solution(mesh):
    in_specs = (
        P("dev", None),
        P("dev", None),
        P(("grp", "dev"), None),
        P(("grp", "dev"), None),
        P(),
    )
    out_specs = (P(("grp", "dev"), None), P())
    return jax.shard_map(body, mesh=mesh, in_specs=in_specs, out_specs=out_specs, check_vma=False)
```

time: 276 us -> 67.6 us (0.24)
  the two profiles are of different devices: /device:TPU:2 before, /device:TPU:1 now
where the time goes in v1:
time: 67.6 us; the launch traced here: 67.5 us
  Pallas kernels  64.1 us (95%)
  local copies, waits for them, and re-layouts  2.72 us (4%)
    pallas_call x1, Pallas kernels, body(): pl.pallas_call(kernel, name='regression_steps', out_shape=(jax.ShapeDtype...  64.1 us
    unnamed x4, local copies, waits for them, and re-layouts  2.72 us

profile of v1, /device:TPU:1, one launch (start us, length us, event | category | flops | bytes accessed | tf_op | source)
XLA Modules:
  0.0 67.5 jit_solution(15738192158683831387)
XLA Ops:
  0.6 64.1 %regression_steps.1 = (f32[512,256]{1,0:T(8,128)}, f32[2,256,256]{2,1,0:T(8,128)}) custom-call(bf16[512,1024]{1,0:T(8,128)(2,1)} %table.1, bf16[512,256]{1,0:T(8,128)(2,1)} %target.1, bf16[512,1024]{1,0:T(8,128)(2,1)} %centres.1, f32[512,256]{1,0:T(8,128)} %coef.1, s32[2,256]{1,0:T(2,128)} %index.1), custom_call_target="tpu_custom_call" | custom-call | tf_op jit(solution)/shard_map/regression_steps/pallas_call | solution.py:280
  64.8 0.0 copy-start
  64.8 1.9 %copy.9 = f32[512,256]{1,0:T(8,128)} copy(f32[512,256]{1,0:T(8,128)} %get-tuple-element.4) | data formatting | bytes 1048576
  66.7 0.0 copy-done
  66.7 0.8 %copy.10 = f32[2,256,256]{2,1,0:T(8,128)} copy(f32[2,256,256]{2,1,0:T(8,128)S(1)} %copy-done) | data formatting | bytes 1048576
Async XLA Ops:
  64.8 1.9 %copy-start = (f32[2,256,256]{2,1,0:T(8,128)S(1)}, f32[2,256,256]{2,1,0:T(8,128)}, u32[]{:S(2)}) copy-start(f32[2,256,256]{2,1,0:T(8,128)} %get-tuple-element.5) | copy-start | bytes 1572868

commit v2 on v1

v2 whole, which is shorter than its diff:
```python
import math

import jax
import jax.numpy as jnp
from jax import lax
from jax.experimental import pallas as pl
from jax.experimental.pallas import tpu as pltpu
from jax.sharding import PartitionSpec as P

MESH = pl.DeviceIdType.MESH
SPREAD = 2.0
RATE = 2.0
NX, NC, NY, NZ = 4, 2, 4, 8
NP = NX * NY
ND = NY * NZ
F32 = jnp.float32
BF16 = jnp.bfloat16
HI = lax.Precision.HIGHEST
NN = (((1,), (0,)), ((), ()))
NT = (((1,), (1,)), ((), ()))
TN = (((0,), (0,)), ((), ()))


def hops(k, n):
    return min(k, n - k)


Z_FAR = sorted(range(1, NZ), key=lambda k: -hops(k, NZ))
Z_NEAR = Z_FAR[::-1]
XY_FAR = sorted(
    [(i, j) for i in range(NX) for j in range(NY) if i or j],
    key=lambda o: -hops(o[0], NX) - hops(o[1], NY),
)
YZ_FAR = sorted(
    [(j, k) for j in range(NY) for k in range(NZ) if j or k],
    key=lambda o: -hops(o[0], NY) - hops(o[1], NZ),
)


def dot(a, b, dims=NN, precision=None):
    return lax.dot_general(a, b, dims, precision=precision, preferred_element_type=F32)


def split(a):
    high = a.astype(BF16)
    return high, (a - high.astype(F32)).astype(BF16)


def exchange(
    table, target, centres, coef, index,
    whole, mass_out, wt_high, wt_low,
    tab_v, tgt_v, cen_v, cf_v, idx_v, aims_v, cf_high, cf_low,
    pick, parts, rows,
    w_high, w_low, core_send, core_recv, xy_send, xy_recv, z_buf,
    load_sem, sent, a_recv, az_recv, axy_recv, ac_recv,
    cc_send, cc_recv, cxy_recv, cz_recv, gxy_recv, gc_recv,
):
    g = lax.axis_index("grp")
    d = lax.axis_index("dev")
    x, c = g // 2, g % 2
    y, z = d // NZ, d % NZ
    p = x * NY + y
    feat = c * NX + x
    chunk = z * NY + y
    radius = math.sqrt(2.0 * 1024)
    scale = 1.0 / math.sqrt(131072)

    xs = [lax.rem(x + k, NX) for k in range(NX)]
    ys = [lax.rem(y + k, NY) for k in range(NY)]
    zs = [lax.rem(z + k, NZ) for k in range(NZ)]
    grps = [v * 2 + c for v in xs]
    bases = [v * NZ for v in ys]

    def at_xy(o):
        return {"grp": grps[o[0]], "dev": bases[o[1]] + z}

    def at_yz(o):
        return {"grp": g, "dev": bases[o[0]] + zs[o[1]]}

    sibling = {"grp": x * 2 + 1 - c, "dev": d}

    def send(src, dst, send_sem, recv_sem, to):
        copy = pltpu.make_async_remote_copy(
            src_ref=src, dst_ref=dst, send_sem=send_sem, recv_sem=recv_sem,
            device_id=to, device_id_type=MESH,
        )
        copy.start()
        return copy

    def wait_bytes(ref, sem):
        pltpu.make_async_copy(ref, ref, sem).wait()

    barrier = pltpu.get_barrier_semaphore()
    greeted = [at_yz(o) for o in YZ_FAR] + [at_xy(o) for o in XY_FAR if o[0]] + [sibling]
    for to in greeted:
        pl.semaphore_signal(barrier, inc=1, device_id=to, device_id_type=MESH)

    loads = [
        pltpu.make_async_copy(index, idx_v, load_sem.at[0]),
        pltpu.make_async_copy(
            table.at[:, pl.ds(pl.multiple_of(feat * 128, 128), 128)], tab_v, load_sem.at[1]
        ),
        pltpu.make_async_copy(target, tgt_v, load_sem.at[2]),
        pltpu.make_async_copy(centres, cen_v, load_sem.at[3]),
        pltpu.make_async_copy(coef, cf_v, load_sem.at[4]),
    ]
    for load in loads:
        load.start()

    loads[0].wait()
    here = lax.broadcasted_iota(jnp.int32, (512, 256), 0) + d * 512
    hot = jnp.concatenate(
        [(here == idx_v[s : s + 1, :]).astype(F32).astype(BF16) for s in range(2)], axis=1
    )
    loads[1].wait()
    pick[...] = dot(hot, tab_v[...], TN).astype(BF16).reshape(ND, 16, 128)
    parts[chunk] = pick[chunk]

    pl.semaphore_wait(barrier, len(greeted))

    for o in YZ_FAR:
        send(
            pick.at[zs[o[1]] * NY + ys[o[0]]], parts.at[chunk], sent.at[0], a_recv, at_yz(o)
        )

    loads[2].wait()
    first = (g == 0).astype(F32)
    aims_v[...] = dot(hot, tgt_v[...], TN) * first
    loads[3].wait()
    high, low = split(jnp.square(cen_v[...].astype(F32)))
    ones = jnp.ones((8, 1024), BF16)
    cnorm = (dot(ones, high, NT) + dot(ones, low, NT))[0:1, :]
    loads[4].wait()
    cf_high[...], cf_low[...] = split(cf_v[...])

    wait_bytes(parts.at[pl.ds(0, ND - 1)], a_recv)
    own = jnp.sum(parts[...].astype(F32), axis=0).astype(BF16)
    lane = pl.ds(pl.multiple_of(feat * 128, 128), 128)
    rows[pl.ds(pl.multiple_of(chunk * 16, 16), 16), lane] = own

    def block(zz):
        return rows.at[pl.ds(pl.multiple_of((zz * NY + y) * 16, 16), 16), lane]

    for k in Z_FAR:
        send(block(z), block(z), sent.at[1], az_recv.at[k], at_yz((0, k)))

    def pass_on(k):
        there = block(zs[(NZ - k) % NZ])
        for o in XY_FAR:
            send(there, there, sent.at[2], axy_recv.at[k], at_xy(o))

    pass_on(0)
    for k in Z_NEAR:
        wait_bytes(block(z), az_recv.at[k])
        pass_on(k)

    half = pl.ds(pl.multiple_of(c * 512, 512), 512)
    for k in [0] + Z_NEAR:
        wait_bytes(parts.at[pl.ds(0, NP - 1)], axy_recv.at[k])
        strip = rows.at[pl.ds(pl.multiple_of(zs[(NZ - k) % NZ] * 64, 64), 64), half]
        send(strip, strip, sent.at[3], ac_recv, sibling)
    wait_bytes(rows.at[:, pl.ds(0, 512)], ac_recv)

    all_rows = rows[...]
    rnorm = jnp.sum(jnp.square(all_rows.astype(F32)), axis=1, keepdims=True)
    cross = dot(all_rows, cen_v[...], NT)
    dist = jnp.sqrt(jnp.maximum(rnorm + cnorm - 2.0 * cross, 0.0))
    w_high[...], w_low[...] = split(jnp.exp((radius - dist) / SPREAD) * scale)

    ones = jnp.ones((8, 512), BF16)
    mass = dot(ones, w_high[...], NT) + dot(ones, w_low[...], NT)
    mass = jnp.concatenate(
        [mass[0:1, n * 128 : n * 128 + 128] for n in range(4)] + [jnp.zeros((4, 128), F32)], axis=0
    )

    def partials(h, dst):
        r0 = pl.ds(pl.multiple_of(h * 128, 128), 128)
        r1 = pl.ds(pl.multiple_of(h * 128 + 256, 128), 128)
        h0, l0, h1, l1 = w_high[r0, :], w_low[r0, :], w_high[r1, :], w_low[r1, :]
        ch, cl = cf_high[...], cf_low[...]
        gh, gl = w_high[0:256, :], w_low[0:256, :]
        s0 = dot(h0, ch) + (dot(h0, cl) + dot(l0, ch)) - aims_v[r0, :]
        s1 = dot(h1, ch) + (dot(h1, cl) + dot(l1, ch)) - aims_v[r1, :]
        gram = dot(h1, gh, NT) + (dot(h1, gl, NT) + dot(l1, gh, NT))
        for n, part in enumerate((s0, s1, gram)):
            for m in range(2):
                at = n * 16 + m * 8
                dst[:, at : at + 8, :] = part[:, m * 128 : m * 128 + 128].reshape(NP, 8, 128)
        dst[:, 48:56, :] = jnp.broadcast_to(mass[None], (NP, 8, 128))

    partials(1 - c, core_send)
    core_copy = send(core_send, core_recv, cc_send, cc_recv, sibling)
    partials(c, xy_send)
    core_copy.wait()
    xy_send[...] = xy_send[...] + core_recv[...]

    for o in XY_FAR:
        send(
            xy_send.at[xs[o[0]] * NY + ys[o[1]]], xy_recv.at[p], sent.at[4], cxy_recv, at_xy(o)
        )
    xy_recv[p] = xy_send[p]
    wt_high[...] = w_high[...].T
    wt_low[...] = w_low[...].T
    wait_bytes(xy_recv.at[pl.ds(0, NP - 1)], cxy_recv)
    z_buf[z] = jnp.sum(xy_recv[...], axis=0)

    for k in Z_FAR:
        send(z_buf.at[z], z_buf.at[z], sent.at[5], cz_recv, at_yz((0, k)))
    wait_bytes(z_buf.at[pl.ds(0, NZ - 1)], cz_recv)
    total = jnp.sum(z_buf[...], axis=0)
    whole[c, p] = total[0:48]

    for o in XY_FAR:
        send(whole.at[c, p], whole.at[c, p], sent.at[6], gxy_recv, at_xy(o))
    mass_out[...] = total[48:56]
    wait_bytes(whole.at[0, pl.ds(0, NP - 1)], gxy_recv)
    send(whole.at[c], whole.at[c], sent.at[7], gc_recv, sibling)
    wait_bytes(whole.at[0], gc_recv)

    wait_bytes(parts.at[pl.ds(0, ND - 1)], sent.at[0])
    wait_bytes(parts.at[pl.ds(0, NZ - 1)], sent.at[1])
    wait_bytes(rows.at[pl.ds(0, 480), pl.ds(0, 512)], sent.at[2])
    wait_bytes(rows.at[:, pl.ds(0, 512)], sent.at[3])
    wait_bytes(xy_recv.at[pl.ds(0, NP - 1)], sent.at[4])
    wait_bytes(z_buf.at[pl.ds(0, NZ - 1)], sent.at[5])
    wait_bytes(whole.at[0, pl.ds(0, NP - 1)], sent.at[6])
    wait_bytes(whole.at[0], sent.at[7])


def update(whole, mass, wt_high, wt_low, coef, coef_out, resid_out):
    def piece(n):
        halves = [
            jnp.concatenate(
                [whole[h, :, n * 16 + m * 8 : n * 16 + m * 8 + 8, :].reshape(128, 128) for m in range(2)],
                axis=1,
            )
            for h in range(2)
        ]
        return jnp.concatenate(halves, axis=0)

    def column(s):
        tiles = [jnp.broadcast_to(mass[2 * s + m : 2 * s + m + 1, :], (128, 128)).T for m in range(2)]
        tall = jnp.concatenate(tiles, axis=0)
        return jnp.concatenate([tall, tall], axis=1)

    def project(resid, m):
        along = jnp.sum(m * resid, axis=0, keepdims=True) / jnp.sum(m * m, axis=0, keepdims=True)
        return resid - m * along

    def grad(s, proj):
        ph, pw = split(proj)
        th, tl = wt_high[:, s * 256 : s * 256 + 256], wt_low[:, s * 256 : s * 256 + 256]
        return dot(th, ph) + (dot(th, pw) + dot(tl, ph))

    m0, m1 = column(0), column(1)
    resid0 = piece(0)
    resid_out[0] = resid0
    proj0 = project(resid0, m0)
    resid1 = piece(1) - RATE * dot(piece(2), proj0, precision=HI)
    resid_out[1] = resid1
    step0 = grad(0, proj0)
    proj1 = project(resid1, m1)
    coef_out[...] = coef[...] - RATE * (step0 + grad(1, proj1))


def body(table, target_table, centres, coefficients, batch_index):
    dma = pltpu.SemaphoreType.DMA
    vmem = pl.BlockSpec(memory_space=pltpu.VMEM)
    sums = pl.pallas_call(
        exchange,
        name="exchange",
        out_shape=(
            jax.ShapeDtypeStruct((2, NP, 48, 128), F32),
            jax.ShapeDtypeStruct((8, 128), F32),
            jax.ShapeDtypeStruct((512, 512), BF16),
            jax.ShapeDtypeStruct((512, 512), BF16),
        ),
        in_specs=[pl.BlockSpec(memory_space=pltpu.HBM)] * 5,
        out_specs=(vmem,) * 4,
        scratch_shapes=[
            pltpu.VMEM((512, 128), BF16),
            pltpu.VMEM((512, 256), BF16),
            pltpu.VMEM((512, 1024), BF16),
            pltpu.VMEM((512, 256), F32),
            pltpu.VMEM((2, 256), jnp.int32),
            pltpu.VMEM((512, 256), F32),
            pltpu.VMEM((512, 256), BF16),
            pltpu.VMEM((512, 256), BF16),
            pltpu.VMEM((ND, 16, 128), BF16),
            pltpu.VMEM((ND, 16, 128), BF16),
            pltpu.VMEM((512, 1024), BF16),
            pltpu.VMEM((512, 512), BF16),
            pltpu.VMEM((512, 512), BF16),
            pltpu.VMEM((NP, 56, 128), F32),
            pltpu.VMEM((NP, 56, 128), F32),
            pltpu.VMEM((NP, 56, 128), F32),
            pltpu.VMEM((NP, 56, 128), F32),
            pltpu.VMEM((NZ, 56, 128), F32),
            dma((5,)), dma((8,)), dma, dma((NZ,)), dma((NZ,)), dma,
            dma, dma, dma, dma, dma, dma,
        ],
        compiler_params=pltpu.CompilerParams(
            collective_id=0, has_side_effects=True, vmem_limit_bytes=40 * 2**20
        ),
    )(table, target_table, centres, coefficients, batch_index)
    return pl.pallas_call(
        update,
        name="update",
        out_shape=(
            jax.ShapeDtypeStruct((512, 256), F32),
            jax.ShapeDtypeStruct((2, 256, 256), F32),
        ),
        in_specs=[vmem] * 5,
        out_specs=(vmem, vmem),
        compiler_params=pltpu.CompilerParams(vmem_limit_bytes=24 * 2**20),
    )(*sums, coefficients)


def solution(mesh):
    in_specs = (
        P("dev", None),
        P("dev", None),
        P(("grp", "dev"), None),
        P(("grp", "dev"), None),
        P(),
    )
    out_specs = (P(("grp", "dev"), None), P())
    return jax.shard_map(body, mesh=mesh, in_specs=in_specs, out_specs=out_specs, check_vma=False)
```

time: 67.6 us -> 63.7 us (0.942)
  Pallas kernels: 64.1 us -> 57.7 us
  local copies, waits for them, and re-layouts: 2.72 us -> 5.11 us
    pallas_call x1 -> x2, Pallas kernels: 64.1 us -> 57.7 us  [the longest x1 55.6 us: body(): pl.pallas_call(exchange, name='exchange', out_shape=(jax.ShapeDtypeStruct...]
    unnamed x4 -> x10, local copies, waits for them, and re-layouts: 2.72 us -> 5.11 us
where the time goes in v2:
time: 63.7 us; the launch traced here: 63.5 us
  Pallas kernels  57.7 us (91%)
  local copies, waits for them, and re-layouts  5.11 us (8%)
  between operations  0.65 us (1%)
    pallas_call x1, Pallas kernels, body(): pl.pallas_call(exchange, name='exchange', out_shape=(jax.ShapeDtypeStruct...  55.6 us
    unnamed x10, local copies, waits for them, and re-layouts  5.11 us
    pallas_call x1, Pallas kernels, body(): pl.pallas_call(update, name='update', out_shape=(jax.ShapeDtypeStruct((51...  2.13 us

profile of v2, /device:TPU:1, one launch (start us, length us, event | category | flops | bytes accessed | tf_op | source)
XLA Modules:
  0.0 63.5 jit_solution(2077070925218051376)
XLA Ops:
  0.6 0.0 copy-start
  0.6 1.0 %copy-done = f32[512,256]{1,0:T(8,128)S(1)} copy-done((f32[512,256]{1,0:T(8,128)S(1)}, f32[512,256]{1,0:T(8,128)}, u32[]{:S(2)}) %copy-start) | copy-done | bytes 524312
  1.7 0.0 copy-start.1
  1.7 1.2 %copy-done.1 = bf16[512,1024]{1,0:T(8,128)(2,1)S(1)} copy-done((bf16[512,1024]{1,0:T(8,128)(2,1)S(1)}, bf16[512,1024]{1,0:T(8,128)(2,1)}, u32[]{:S(2)}) %copy-start.1) | copy-done | bytes 1048600
  2.9 0.0 copy-start.2
  2.9 1.2 %copy-done.2 = bf16[512,1024]{1,0:T(8,128)(2,1)S(1)} copy-done((bf16[512,1024]{1,0:T(8,128)(2,1)S(1)}, bf16[512,1024]{1,0:T(8,128)(2,1)}, u32[]{:S(2)}) %copy-start.2) | copy-done | bytes 1048600
  4.1 0.0 copy-start.3
  4.1 0.9 %copy-done.3 = bf16[512,256]{1,0:T(8,128)(2,1)S(1)} copy-done((bf16[512,256]{1,0:T(8,128)(2,1)S(1)}, bf16[512,256]{1,0:T(8,128)(2,1)}, u32[]{:S(2)}) %copy-start.3) | copy-done | bytes 262168
  5.1 0.0 copy-start.4
  5.1 0.7 %copy-done.4 = s32[2,256]{1,0:T(2,128)S(1)} copy-done((s32[2,256]{1,0:T(2,128)S(1)}, s32[2,256]{1,0:T(2,128)}, u32[]{:S(2)}) %copy-start.4) | copy-done | bytes 2072
  5.8 55.6 %exchange.1 = (f32[2,16,48,128]{3,2,1,0:T(8,128)S(1)}, f32[8,128]{1,0:T(8,128)S(1)}, bf16[512,512]{1,0:T(8,128)(2,1)S(1)}, bf16[512,512]{1,0:T(8,128)(2,1)S(1)}) custom-call(bf16[512,1024]{1,0:T(8,128)(2,1)S(1)} %copy-done.1, bf16[512,256]{1,0:T(8,128)(2,1)S(1)} %copy-done.3, bf16[512,1024]{1,0:T(8,128)(2,1)S(1)} %copy-done.2, f32[512,256]{1,0:T(8,128)S(1)} %copy-done, ...), custom_call_target="tpu_custom_call" | custom-call | tf_op jit(solution)/shard_map/exchange/pallas_call | solution.py:269
  61.4 2.1 %update.1 = (f32[512,256]{1,0:T(8,128)}, f32[2,256,256]{2,1,0:T(8,128)}) custom-call(f32[2,16,48,128]{3,2,1,0:T(8,128)S(1)} %get-tuple-element.6.whole, f32[8,128]{1,0:T(8,128)S(1)} %get-tuple-element.7.mass, bf16[512,512]{1,0:T(8,128)(2,1)S(1)} %get-tuple-element.8.wt_high, bf16[512,512]{1,0:T(8,128)(2,1)S(1)} %get-tuple-element.9.wt_low, ...), custom_call_target="tpu_custom_call" | custom-call | tf_op jit(solution)/shard_map/update/pallas_call | solution.py:306
Async XLA Ops:
  0.6 1.0 %copy-start = (f32[512,256]{1,0:T(8,128)S(1)}, f32[512,256]{1,0:T(8,128)}, u32[]{:S(2)}) copy-start(f32[512,256]{1,0:T(8,128)} %coef.3) | copy-start | bytes 1572868
  1.7 1.2 %copy-start.1 = (bf16[512,1024]{1,0:T(8,128)(2,1)S(1)}, bf16[512,1024]{1,0:T(8,128)(2,1)}, u32[]{:S(2)}) copy-start(bf16[512,1024]{1,0:T(8,128)(2,1)} %table.1) | copy-start | bytes 3145732
  2.9 1.2 %copy-start.2 = (bf16[512,1024]{1,0:T(8,128)(2,1)S(1)}, bf16[512,1024]{1,0:T(8,128)(2,1)}, u32[]{:S(2)}) copy-start(bf16[512,1024]{1,0:T(8,128)(2,1)} %centres.1) | copy-start | bytes 3145732
  4.1 0.9 %copy-start.3 = (bf16[512,256]{1,0:T(8,128)(2,1)S(1)}, bf16[512,256]{1,0:T(8,128)(2,1)}, u32[]{:S(2)}) copy-start(bf16[512,256]{1,0:T(8,128)(2,1)} %target.1) | copy-start | bytes 786436
  5.1 0.7 %copy-start.4 = (s32[2,256]{1,0:T(2,128)S(1)}, s32[2,256]{1,0:T(2,128)}, u32[]{:S(2)}) copy-start(s32[2,256]{1,0:T(2,128)} %index.1) | copy-start | bytes 6148

commit v3 on v2

--- a/solution.py
+++ b/solution.py
@@ -302,7 +302,10 @@
         compiler_params=pltpu.CompilerParams(
             collective_id=0, has_side_effects=True, vmem_limit_bytes=40 * 2**20
         ),
-    )(table, target_table, centres, coefficients, batch_index)
+    )(*[
+        pltpu.with_memory_space_constraint(a, pltpu.HBM)
+        for a in (table, target_table, centres, coefficients, batch_index)
+    ])
     return pl.pallas_call(
         update,
         name="update",

time: 63.7 us -> 58.8 us (0.923)
  local copies, waits for them, and re-layouts: 5.11 us -> 0.01 us
    unnamed x10 -> x2, local copies, waits for them, and re-layouts: 5.11 us -> 0.01 us
where the time goes in v3:
time: 58.8 us; the launch traced here: 58.7 us
  Pallas kernels  58.1 us (99%)
  between operations  0.65 us (1%)
    pallas_call x1, Pallas kernels, body(): pl.pallas_call(exchange, name='exchange', out_shape=(jax.ShapeDtypeStruct...  55.9 us
    pallas_call x1, Pallas kernels, body(): pl.pallas_call(update, name='update', out_shape=(jax.ShapeDtypeStruct((51...  2.13 us

profile of v3, /device:TPU:1, one launch (start us, length us, event | category | flops | bytes accessed | tf_op | source)
XLA Modules:
  0.0 58.7 jit_solution(13957239172281749014)
XLA Ops:
  0.6 0.0 copy-start
  0.6 55.9 %exchange.1 = (f32[2,16,48,128]{3,2,1,0:T(8,128)S(1)}, f32[8,128]{1,0:T(8,128)S(1)}, bf16[512,512]{1,0:T(8,128)(2,1)S(1)}, bf16[512,512]{1,0:T(8,128)(2,1)S(1)}) custom-call(bf16[512,1024]{1,0:T(8,128)(2,1)} %table.1, bf16[512,256]{1,0:T(8,128)(2,1)} %target.1, bf16[512,1024]{1,0:T(8,128)(2,1)} %centres.1, f32[512,256]{1,0:T(8,128)} %coef.3, s32[2,256]{1,0:T(2,128)} %index.1), custom_call_target="tpu_custom_call" | custom-call | tf_op jit(solution)/shard_map/exchange/pallas_call | solution.py:269
  56.6 0.0 copy-done
  56.6 2.1 %update.1 = (f32[512,256]{1,0:T(8,128)}, f32[2,256,256]{2,1,0:T(8,128)}) custom-call(f32[2,16,48,128]{3,2,1,0:T(8,128)S(1)} %get-tuple-element.6.whole, f32[8,128]{1,0:T(8,128)S(1)} %get-tuple-element.7.mass, bf16[512,512]{1,0:T(8,128)(2,1)S(1)} %get-tuple-element.8.wt_high, bf16[512,512]{1,0:T(8,128)(2,1)S(1)} %get-tuple-element.9.wt_low, ...), custom_call_target="tpu_custom_call" | custom-call | tf_op jit(solution)/shard_map/update/pallas_call | solution.py:309
Async XLA Ops:
  0.6 56.0 %copy-start = (f32[512,256]{1,0:T(8,128)S(1)}, f32[512,256]{1,0:T(8,128)}, u32[]{:S(2)}) copy-start(f32[512,256]{1,0:T(8,128)} %coef.3) | copy-start | bytes 1572868

commit v4 on v3

v4 whole, which is shorter than its diff:
```python
import math

import jax
import jax.numpy as jnp
from jax import lax
from jax.experimental import pallas as pl
from jax.experimental.pallas import tpu as pltpu
from jax.sharding import PartitionSpec as P

MESH = pl.DeviceIdType.MESH
SPREAD = 2.0
RATE = 2.0
NX, NC, NY, NZ = 4, 2, 4, 8
NP = NX * NY
ND = NY * NZ
F32 = jnp.float32
BF16 = jnp.bfloat16
HI = lax.Precision.HIGHEST
NN = (((1,), (0,)), ((), ()))
NT = (((1,), (1,)), ((), ()))
TN = (((0,), (0,)), ((), ()))


def hops(k, n):
    return min(k, n - k)


Z_FAR = sorted(range(1, NZ), key=lambda k: -hops(k, NZ))
Z_NEAR = Z_FAR[::-1]
XY_FAR = sorted(
    [(i, j) for i in range(NX) for j in range(NY) if i or j],
    key=lambda o: -hops(o[0], NX) - hops(o[1], NY),
)
YZ_FAR = sorted(
    [(j, k) for j in range(NY) for k in range(NZ) if j or k],
    key=lambda o: -hops(o[0], NY) - hops(o[1], NZ),
)


def dot(a, b, dims=NN, precision=None):
    return lax.dot_general(a, b, dims, precision=precision, preferred_element_type=F32)


def split(a):
    high = a.astype(BF16)
    return high, (a - high.astype(F32)).astype(BF16)


SLOTS = [0, 1, 7, 2, 6, 3, 5, 4]
GROUPS = [(0, 3), (3, 7), (7, 8)]
SHARE = (16, 24, 16)


def pieces_to_whole(whole):
    halves = [
        jnp.concatenate([whole[h, :, m * 8 : m * 8 + 8, :].reshape(128, 128) for m in range(2)], axis=1)
        for h in range(2)
    ]
    return jnp.concatenate(halves, axis=0)


def column(mass, s):
    tiles = [jnp.broadcast_to(mass[2 * s + m : 2 * s + m + 1, :], (128, 128)).T for m in range(2)]
    tall = jnp.concatenate(tiles, axis=0)
    return jnp.concatenate([tall, tall], axis=1)


def project(resid, m):
    along = jnp.sum(m * resid, axis=0, keepdims=True) / jnp.sum(m * m, axis=0, keepdims=True)
    return resid - m * along


def grad(high, low, proj):
    ph, pw = split(proj)
    return dot(high, ph) + (dot(high, pw) + dot(low, ph))


def exchange(
    table, target, centres, coef, index,
    whole2, turn_out, mass_out, wt_high, wt_low, coef_half, resid0_out,
    tab_v, tgt_v, cen_v, cf_v, idx_v, aims_v, cf_high, cf_low,
    pick, parts, rows, w_high, w_low, wt0_high, wt0_low,
    core_send0, core_send1, core_send2, core_recv0, core_recv1, core_recv2,
    xy_send0, xy_send1, xy_send2, xy_recv0, xy_recv1, xy_recv2,
    z_buf0, z_buf1, z_buf2, whole0, whole1,
    load_sem, a_sent, a_recv, az_recv, axy_recv, ac_recv,
    c_sent, cc_recv, cxy_recv, cz_recv, gxy_recv, gc_recv,
):
    core_send, core_recv = (core_send0, core_send1, core_send2), (core_recv0, core_recv1, core_recv2)
    xy_send, xy_recv = (xy_send0, xy_send1, xy_send2), (xy_recv0, xy_recv1, xy_recv2)
    z_buf, whole = (z_buf0, z_buf1, z_buf2), (whole0, whole1, whole2)
    g = lax.axis_index("grp")
    d = lax.axis_index("dev")
    x, c = g // 2, g % 2
    y, z = d // NZ, d % NZ
    p = x * NY + y
    feat = c * NX + x
    chunk = z * NY + y
    radius = math.sqrt(2.0 * 1024)
    scale = 1.0 / math.sqrt(131072)

    xs = [lax.rem(x + k, NX) for k in range(NX)]
    ys = [lax.rem(y + k, NY) for k in range(NY)]
    zs = [lax.rem(z + k, NZ) for k in range(NZ)]
    grps = [v * 2 + c for v in xs]
    bases = [v * NZ for v in ys]

    def at_xy(o):
        return {"grp": grps[o[0]], "dev": bases[o[1]] + z}

    def at_yz(o):
        return {"grp": g, "dev": bases[o[0]] + zs[o[1]]}

    sibling = {"grp": x * 2 + 1 - c, "dev": d}

    def send(src, dst, send_sem, recv_sem, to):
        copy = pltpu.make_async_remote_copy(
            src_ref=src, dst_ref=dst, send_sem=send_sem, recv_sem=recv_sem,
            device_id=to, device_id_type=MESH,
        )
        copy.start()
        return copy

    def wait_bytes(ref, sem):
        pltpu.make_async_copy(ref, ref, sem).wait()

    barrier = pltpu.get_barrier_semaphore()
    greeted = [at_yz(o) for o in YZ_FAR] + [at_xy(o) for o in XY_FAR if o[0]] + [sibling]
    for to in greeted:
        pl.semaphore_signal(barrier, inc=1, device_id=to, device_id_type=MESH)

    loads = [
        pltpu.make_async_copy(index, idx_v, load_sem.at[0]),
        pltpu.make_async_copy(
            table.at[:, pl.ds(pl.multiple_of(feat * 128, 128), 128)], tab_v, load_sem.at[1]
        ),
        pltpu.make_async_copy(target, tgt_v, load_sem.at[2]),
        pltpu.make_async_copy(centres, cen_v, load_sem.at[3]),
        pltpu.make_async_copy(coef, cf_v, load_sem.at[4]),
    ]
    for load in loads:
        load.start()

    loads[0].wait()
    here = lax.broadcasted_iota(jnp.int32, (512, 256), 0) + d * 512
    hot = jnp.concatenate(
        [(here == idx_v[s : s + 1, :]).astype(F32).astype(BF16) for s in range(2)], axis=1
    )
    loads[1].wait()
    pick[...] = dot(hot, tab_v[...], TN).astype(BF16).reshape(ND, 16, 128)
    parts[chunk] = pick[chunk]

    pl.semaphore_wait(barrier, len(greeted))

    for o in YZ_FAR:
        send(
            pick.at[zs[o[1]] * NY + ys[o[0]]], parts.at[chunk], a_sent.at[0], a_recv, at_yz(o)
        )

    loads[2].wait()
    first = (g == 0).astype(F32)
    aims_v[...] = dot(hot, tgt_v[...], TN) * first

    wait_bytes(parts.at[pl.ds(0, ND - 1)], a_recv)
    own = jnp.sum(parts[...].astype(F32), axis=0).astype(BF16)
    lane = pl.ds(pl.multiple_of(feat * 128, 128), 128)
    rows[0, y, :, lane] = own

    mine = rows.at[0, y, :, lane]
    for k in Z_FAR:
        there = rows.at[SLOTS.index(NZ - k), y, :, lane]
        send(mine, there, a_sent.at[1], az_recv.at[NZ - k], at_yz((0, k)))
    for n, (b, e) in enumerate(GROUPS):
        for r in SLOTS[b:e]:
            if r:
                wait_bytes(parts.at[0], az_recv.at[r])
        group = rows.at[pl.ds(b, e - b), y, :, lane]
        for o in XY_FAR:
            send(group, group, a_sent.at[2], axy_recv.at[n], at_xy(o))

    loads[3].wait()
    high, low = split(jnp.square(cen_v[...].astype(F32)))
    ones = jnp.ones((8, 1024), BF16)
    cnorm = (dot(ones, high, NT) + dot(ones, low, NT))[0:1, :]
    loads[4].wait()
    cf_high[...], cf_low[...] = split(cf_v[...])

    half = pl.ds(pl.multiple_of(c * 512, 512), 512)
    for n, (b, e) in enumerate(GROUPS):
        wait_bytes(rows.at[pl.ds(0, e - b), pl.ds(0, 3), :, pl.ds(0, 640)], axy_recv.at[n])
        strip = rows.at[pl.ds(b, e - b), :, :, half]
        send(strip, strip, a_sent.at[3], ac_recv.at[n], sibling)

    for n, (b, e) in enumerate(GROUPS):
        wait_bytes(rows.at[pl.ds(0, e - b), :, :, pl.ds(0, 512)], ac_recv.at[n])
        some = rows[b:e].reshape((e - b) * 64, 1024)
        rnorm = jnp.sum(jnp.square(some.astype(F32)), axis=1, keepdims=True)
        cross = dot(some, cen_v[...], NT)
        dist = jnp.sqrt(jnp.maximum(rnorm + cnorm - 2.0 * cross, 0.0))
        high, low = split(jnp.exp((radius - dist) / SPREAD) * scale)
        for r in range(b, e):
            at = pl.ds(pl.multiple_of(zs[SLOTS[r]] * 64, 64), 64)
            w_high[at, :] = high[(r - b) * 64 : (r - b) * 64 + 64]
            w_low[at, :] = low[(r - b) * 64 : (r - b) * 64 + 64]

    def terms(n, h, dst):
        s = n // 2
        at = pl.ds(pl.multiple_of(h * 128 + (0, 256, 256)[n], 128), 128)
        high, low = w_high[at, :], w_low[at, :]
        if n == 1:
            gh, gl = w_high[0:256, :], w_low[0:256, :]
            part = dot(high, gh, NT) + (dot(high, gl, NT) + dot(low, gh, NT))
        else:
            ch, cl = cf_high[...], cf_low[...]
            part = dot(high, ch) + (dot(high, cl) + dot(low, ch)) - aims_v[at, :]
        for m in range(2):
            dst[:, m * 8 : m * 8 + 8, :] = part[:, m * 128 : m * 128 + 128].reshape(NP, 8, 128)

    for n in range(3):
        terms(n, 1 - c, core_send[n])
        if n == 1:
            ones = jnp.ones((8, 512), BF16)
            mass = dot(ones, w_high[...], NT) + dot(ones, w_low[...], NT)
            mass = jnp.concatenate(
                [mass[0:1, m * 128 : m * 128 + 128] for m in range(4)] + [jnp.zeros((4, 128), F32)],
                axis=0,
            )
            mass = jnp.broadcast_to(mass[None], (NP, 8, 128))
            core_send[1][:, 16:24, :] = mass
            xy_send[1][:, 16:24, :] = mass
        send(core_send[n], core_recv[n], c_sent.at[n], cc_recv.at[n], sibling)
    for n in range(3):
        terms(n, c, xy_send[n])
        wait_bytes(core_recv[n], cc_recv.at[n])
        xy_send[n][...] = xy_send[n][...] + core_recv[n][...]
        for o in XY_FAR:
            send(
                xy_send[n].at[xs[o[0]] * NY + ys[o[1]]], xy_recv[n].at[p],
                c_sent.at[3 + n], cxy_recv.at[n], at_xy(o),
            )
        xy_recv[n][p] = xy_send[n][p]

    wt0_high[...] = w_high[0:256, :].T
    wt0_low[...] = w_low[0:256, :].T
    wt_high[...] = w_high[256:512, :].T
    wt_low[...] = w_low[256:512, :].T

    for n in range(3):
        wait_bytes(xy_recv[n].at[pl.ds(0, NP - 1)], cxy_recv.at[n])
        z_buf[n][z] = jnp.sum(xy_recv[n][...], axis=0)
        for k in Z_FAR:
            send(z_buf[n].at[z], z_buf[n].at[z], c_sent.at[6 + n], cz_recv.at[n], at_yz((0, k)))
    for n in range(3):
        wait_bytes(z_buf[n].at[pl.ds(0, NZ - 1)], cz_recv.at[n])
        total = jnp.sum(z_buf[n][...], axis=0)
        whole[n][c, p] = total[0:16]
        for o in XY_FAR:
            send(whole[n].at[c, p], whole[n].at[c, p], c_sent.at[9 + n], gxy_recv.at[n], at_xy(o))
        if n == 1:
            mass = total[16:24]
            mass_out[...] = mass
            m0 = column(mass, 0)
    for n in range(3):
        wait_bytes(whole[n].at[0, pl.ds(0, NP - 1)], gxy_recv.at[n])
        send(whole[n].at[c], whole[n].at[c], c_sent.at[12 + n], gc_recv.at[n], sibling)

    wait_bytes(whole[0].at[0], gc_recv.at[0])
    resid0 = pieces_to_whole(whole0)
    resid0_out[...] = resid0
    proj0 = project(resid0, m0)
    wait_bytes(whole[1].at[0], gc_recv.at[1])
    turn_out[...] = RATE * dot(pieces_to_whole(whole1), proj0, precision=HI)
    coef_half[...] = cf_v[...] - RATE * grad(wt0_high[...], wt0_low[...], proj0)
    wait_bytes(whole[2].at[0], gc_recv.at[2])

    wait_bytes(parts.at[pl.ds(0, ND - 1)], a_sent.at[0])
    wait_bytes(parts.at[pl.ds(0, NZ - 1)], a_sent.at[1])
    wait_bytes(rows.at[:, pl.ds(0, 3), :, pl.ds(0, 640)], a_sent.at[2])
    wait_bytes(rows.at[:, :, :, pl.ds(0, 512)], a_sent.at[3])
    for n in range(3):
        wait_bytes(core_recv[n], c_sent.at[n])
        wait_bytes(xy_recv[n].at[pl.ds(0, NP - 1)], c_sent.at[3 + n])
        wait_bytes(z_buf[n].at[pl.ds(0, NZ - 1)], c_sent.at[6 + n])
        wait_bytes(whole[n].at[0, pl.ds(0, NP - 1)], c_sent.at[9 + n])
        wait_bytes(whole[n].at[0], c_sent.at[12 + n])


def update(whole2, turn, mass, wt_high, wt_low, coef_half, resid0, coef_out, resid_out):
    resid1 = pieces_to_whole(whole2) - turn[...]
    resid_out[0] = resid0[...]
    resid_out[1] = resid1
    proj1 = project(resid1, column(mass[...], 1))
    coef_out[...] = coef_half[...] - RATE * grad(wt_high[...], wt_low[...], proj1)


def body(table, target_table, centres, coefficients, batch_index):
    dma = pltpu.SemaphoreType.DMA
    vmem = pl.BlockSpec(memory_space=pltpu.VMEM)
    square = jax.ShapeDtypeStruct((256, 256), F32)
    turned = jax.ShapeDtypeStruct((512, 256), BF16)
    per_peer = [pltpu.VMEM((NP, n, 128), F32) for n in SHARE]
    sums = pl.pallas_call(
        exchange,
        name="exchange",
        out_shape=(
            jax.ShapeDtypeStruct((2, NP, 16, 128), F32),
            square,
            jax.ShapeDtypeStruct((8, 128), F32),
            turned,
            turned,
            jax.ShapeDtypeStruct((512, 256), F32),
            square,
        ),
        in_specs=[pl.BlockSpec(memory_space=pl.ANY)] * 5,
        out_specs=(vmem,) * 7,
        scratch_shapes=[
            pltpu.VMEM((512, 128), BF16),
            pltpu.VMEM((512, 256), BF16),
            pltpu.VMEM((512, 1024), BF16),
            pltpu.VMEM((512, 256), F32),
            pltpu.VMEM((2, 256), jnp.int32),
            pltpu.VMEM((512, 256), F32),
            pltpu.VMEM((512, 256), BF16),
            pltpu.VMEM((512, 256), BF16),
            pltpu.VMEM((ND, 16, 128), BF16),
            pltpu.VMEM((ND, 16, 128), BF16),
            pltpu.VMEM((NZ, NY, 16, 1024), BF16),
            pltpu.VMEM((512, 512), BF16),
            pltpu.VMEM((512, 512), BF16),
            pltpu.VMEM((512, 256), BF16),
            pltpu.VMEM((512, 256), BF16),
            *per_peer, *per_peer, *per_peer, *per_peer,
            *[pltpu.VMEM((NZ, n, 128), F32) for n in SHARE],
            pltpu.VMEM((2, NP, 16, 128), F32),
            pltpu.VMEM((2, NP, 16, 128), F32),
            dma((5,)), dma((4,)), dma, dma((NZ,)), dma((3,)), dma((3,)),
            dma((15,)), dma((3,)), dma((3,)), dma((3,)), dma((3,)), dma((3,)),
        ],
        compiler_params=pltpu.CompilerParams(
            collective_id=0, has_side_effects=True, vmem_limit_bytes=40 * 2**20
        ),
    )(*[
        pltpu.with_memory_space_constraint(a, pltpu.HBM)
        for a in (table, target_table, centres, coefficients, batch_index)
    ])
    return pl.pallas_call(
        update,
        name="update",
        out_shape=(
            jax.ShapeDtypeStruct((512, 256), F32),
            jax.ShapeDtypeStruct((2, 256, 256), F32),
        ),
        in_specs=[vmem] * 7,
        out_specs=(vmem, vmem),
        compiler_params=pltpu.CompilerParams(vmem_limit_bytes=24 * 2**20),
    )(*sums)


def solution(mesh):
    in_specs = (
        P("dev", None),
        P("dev", None),
        P(("grp", "dev"), None),
        P(("grp", "dev"), None),
        P(),
    )
    out_specs = (P(("grp", "dev"), None), P())
    return jax.shard_map(body, mesh=mesh, in_specs=in_specs, out_specs=out_specs, check_vma=False)
```

time: 58.8 us -> 54.2 us (0.922)
  Pallas kernels: 58.1 us -> 53.5 us
    pallas_call x1, Pallas kernels: 55.9 us -> 52.1 us  [body(): pl.pallas_call(exchange, name='exchange', out_shape=(jax.ShapeDtypeStruct...]
    pallas_call x1, Pallas kernels: 2.13 us -> 1.44 us  [body(): pl.pallas_call(update, name='update', out_shape=(jax.ShapeDtypeStruct((51...]
where the time goes in v4:
time: 54.2 us; the launch traced here: 54.1 us
  Pallas kernels  53.5 us (99%)
  between operations  0.64 us (1%)
    pallas_call x1, Pallas kernels, body(): pl.pallas_call(exchange, name='exchange', out_shape=(jax.ShapeDtypeStruct...  52.1 us
    pallas_call x1, Pallas kernels, body(): pl.pallas_call(update, name='update', out_shape=(jax.ShapeDtypeStruct((51...  1.44 us

profile of v4, /device:TPU:1, one launch (start us, length us, event | category | flops | bytes accessed | tf_op | source)
XLA Modules:
  0.0 54.1 jit_solution(8294637007324877337)
XLA Ops:
  0.6 52.1 %exchange.1 = (f32[2,16,16,128]{3,2,1,0:T(8,128)S(1)}, f32[256,256]{1,0:T(8,128)S(1)}, f32[8,128]{1,0:T(8,128)S(1)}, bf16[512,256]{1,0:T(8,128)(2,1)S(1)}, bf16[...) custom-call(bf16[512,1024]{1,0:T(8,128)(2,1)} %table.1, bf16[512,256]{1,0:T(8,128)(2,1)} %target.1, ...), custom_call_target="tpu_custom_call" | custom-call | tf_op jit(solution)/shard_map/exchange/pallas_call | solution.py:302
  52.7 1.4 %update.1 = (f32[512,256]{1,0:T(8,128)}, f32[2,256,256]{2,1,0:T(8,128)}) custom-call(f32[2,16,16,128]{3,2,1,0:T(8,128)S(1)} %get-tuple-element.9.whole2, f32[256,256]{1,0:T(8,128)S(1)} %get-tuple-element.10.turn, f32[8,128]{1,0:T(8,128)S(1)} %get-tuple-element.11.mass, bf16[512,256]{1,0:T(8,128)(2,1)S(1)} %get-tuple-element.12.wt_high, ...), custom_call_target="tpu_custom_call" | custom-call | tf_op jit(solution)/shard_map/update/pallas_call | solution.py:346

commit v5 on v4

--- a/solution.py
+++ b/solution.py
@@ -46,8 +46,8 @@
     return high, (a - high.astype(F32)).astype(BF16)
 
 
-SLOTS = [0, 1, 7, 2, 6, 3, 5, 4]
-GROUPS = [(0, 3), (3, 7), (7, 8)]
+SLOTS = [0, 2, 6, 3, 5, 4, 1, 7]
+GROUPS = [(0, 1), (1, 2), (2, 3), (3, 6)]
 SHARE = (16, 24, 16)
 
 
@@ -124,11 +124,6 @@
     def wait_bytes(ref, sem):
         pltpu.make_async_copy(ref, ref, sem).wait()
 
-    barrier = pltpu.get_barrier_semaphore()
-    greeted = [at_yz(o) for o in YZ_FAR] + [at_xy(o) for o in XY_FAR if o[0]] + [sibling]
-    for to in greeted:
-        pl.semaphore_signal(barrier, inc=1, device_id=to, device_id_type=MESH)
-
     loads = [
         pltpu.make_async_copy(index, idx_v, load_sem.at[0]),
         pltpu.make_async_copy(
@@ -141,6 +136,11 @@
     for load in loads:
         load.start()
 
+    barrier = pltpu.get_barrier_semaphore()
+    greeted = [at_yz(o) for o in YZ_FAR] + [at_xy(o) for o in XY_FAR if o[0]] + [sibling]
+    for to in greeted:
+        pl.semaphore_signal(barrier, inc=1, device_id=to, device_id_type=MESH)
+
     loads[0].wait()
     here = lax.broadcasted_iota(jnp.int32, (512, 256), 0) + d * 512
     hot = jnp.concatenate(
@@ -160,24 +160,6 @@
     loads[2].wait()
     first = (g == 0).astype(F32)
     aims_v[...] = dot(hot, tgt_v[...], TN) * first
-
-    wait_bytes(parts.at[pl.ds(0, ND - 1)], a_recv)
-    own = jnp.sum(parts[...].astype(F32), axis=0).astype(BF16)
-    lane = pl.ds(pl.multiple_of(feat * 128, 128), 128)
-    rows[0, y, :, lane] = own
-
-    mine = rows.at[0, y, :, lane]
-    for k in Z_FAR:
-        there = rows.at[SLOTS.index(NZ - k), y, :, lane]
-        send(mine, there, a_sent.at[1], az_recv.at[NZ - k], at_yz((0, k)))
-    for n, (b, e) in enumerate(GROUPS):
-        for r in SLOTS[b:e]:
-            if r:
-                wait_bytes(parts.at[0], az_recv.at[r])
-        group = rows.at[pl.ds(b, e - b), y, :, lane]
-        for o in XY_FAR:
-            send(group, group, a_sent.at[2], axy_recv.at[n], at_xy(o))
-
     loads[3].wait()
     high, low = split(jnp.square(cen_v[...].astype(F32)))
     ones = jnp.ones((8, 1024), BF16)
@@ -185,15 +167,49 @@
     loads[4].wait()
     cf_high[...], cf_low[...] = split(cf_v[...])
 
-    half = pl.ds(pl.multiple_of(c * 512, 512), 512)
+    wait_bytes(parts.at[pl.ds(0, ND - 1)], a_recv)
+    own = jnp.sum(parts[...].astype(F32), axis=0).astype(BF16)
+    rows[0, feat, y] = own
+
+    mine = rows.at[0, feat, y]
+    for k in Z_FAR:
+        slot = SLOTS.index(NZ - k)
+        if slot < 6:
+            send(mine, rows.at[slot, feat, y], a_sent.at[1], az_recv.at[NZ - k], at_yz((0, k)))
     for n, (b, e) in enumerate(GROUPS):
-        wait_bytes(rows.at[pl.ds(0, e - b), pl.ds(0, 3), :, pl.ds(0, 640)], axy_recv.at[n])
-        strip = rows.at[pl.ds(b, e - b), :, :, half]
+        for r in SLOTS[b:e]:
+            if r:
+                wait_bytes(parts.at[0], az_recv.at[r])
+        group = rows.at[pl.ds(b, e - b), feat, y]
+        for o in XY_FAR:
+            send(group, group, a_sent.at[2], axy_recv.at[n], at_xy(o))
+
+    half = pl.ds(c * NX, NX)
+
+    def to_sibling(b, e, n):
+        strip = rows.at[pl.ds(b, e - b), half]
         send(strip, strip, a_sent.at[3], ac_recv.at[n], sibling)
 
-    for n, (b, e) in enumerate(GROUPS):
-        wait_bytes(rows.at[pl.ds(0, e - b), :, :, pl.ds(0, 512)], ac_recv.at[n])
-        some = rows[b:e].reshape((e - b) * 64, 1024)
+    def wait_group(n):
+        b, e = GROUPS[n]
+        wait_bytes(rows.at[pl.ds(0, e - b), pl.ds(0, 5), pl.ds(0, 3)], axy_recv.at[n])
+        if n == 0:
+            strip = rows.at[0, half]
+            for k, slot in ((1, 7), (7, 6)):
+                send(strip, rows.at[slot, half], a_sent.at[4], az_recv.at[NZ - k], at_yz((0, k)))
+        to_sibling(b, e, n)
+
+    for n in range(3):
+        wait_group(n)
+    for slot in (6, 7):
+        wait_bytes(rows.at[0, pl.ds(0, NX)], az_recv.at[SLOTS[slot]])
+        to_sibling(slot, slot + 1, slot - 2)
+    wait_group(3)
+
+    for b, e, arrivals in ((0, 3, ((0, 1), (1, 1), (2, 1))), (6, 8, ((4, 1), (5, 1))), (3, 6, ((3, 3),))):
+        for n, blocks in arrivals:
+            wait_bytes(rows.at[pl.ds(0, blocks), pl.ds(0, NX)], ac_recv.at[n])
+        some = jnp.concatenate([rows[b:e, f].reshape((e - b) * 64, 128) for f in range(8)], axis=1)
         rnorm = jnp.sum(jnp.square(some.astype(F32)), axis=1, keepdims=True)
         cross = dot(some, cen_v[...], NT)
         dist = jnp.sqrt(jnp.maximum(rnorm + cnorm - 2.0 * cross, 0.0))
@@ -260,23 +276,27 @@
             mass = total[16:24]
             mass_out[...] = mass
             m0 = column(mass, 0)
-    for n in range(3):
+    def whole_to_sibling(n):
         wait_bytes(whole[n].at[0, pl.ds(0, NP - 1)], gxy_recv.at[n])
         send(whole[n].at[c], whole[n].at[c], c_sent.at[12 + n], gc_recv.at[n], sibling)
 
+    whole_to_sibling(0)
+    whole_to_sibling(1)
     wait_bytes(whole[0].at[0], gc_recv.at[0])
     resid0 = pieces_to_whole(whole0)
     resid0_out[...] = resid0
     proj0 = project(resid0, m0)
+    whole_to_sibling(2)
     wait_bytes(whole[1].at[0], gc_recv.at[1])
     turn_out[...] = RATE * dot(pieces_to_whole(whole1), proj0, precision=HI)
     coef_half[...] = cf_v[...] - RATE * grad(wt0_high[...], wt0_low[...], proj0)
     wait_bytes(whole[2].at[0], gc_recv.at[2])
 
     wait_bytes(parts.at[pl.ds(0, ND - 1)], a_sent.at[0])
-    wait_bytes(parts.at[pl.ds(0, NZ - 1)], a_sent.at[1])
-    wait_bytes(rows.at[:, pl.ds(0, 3), :, pl.ds(0, 640)], a_sent.at[2])
-    wait_bytes(rows.at[:, :, :, pl.ds(0, 512)], a_sent.at[3])
+    wait_bytes(parts.at[pl.ds(0, 5)], a_sent.at[1])
+    wait_bytes(rows.at[pl.ds(0, 6), pl.ds(0, 5), pl.ds(0, 3)], a_sent.at[2])
+    wait_bytes(rows.at[:, pl.ds(0, NX)], a_sent.at[3])
+    wait_bytes(rows.at[pl.ds(0, 2), pl.ds(0, NX)], a_sent.at[4])
     for n in range(3):
         wait_bytes(core_recv[n], c_sent.at[n])
         wait_bytes(xy_recv[n].at[pl.ds(0, NP - 1)], c_sent.at[3 + n])
@@ -285,12 +305,23 @@
         wait_bytes(whole[n].at[0], c_sent.at[12 + n])
 
 
-def update(whole2, turn, mass, wt_high, wt_low, coef_half, resid0, coef_out, resid_out):
+def update(
+    whole2, turn, mass, wt_high, wt_low, coef_half, resid0, coef_out, resid_out, coef_v, resid1_v, out_sem
+):
+    copies = [pltpu.make_async_copy(resid0, resid_out.at[0], out_sem.at[0])]
+    copies[0].start()
     resid1 = pieces_to_whole(whole2) - turn[...]
-    resid_out[0] = resid0[...]
-    resid_out[1] = resid1
+    resid1_v[...] = resid1
+    copies.append(pltpu.make_async_copy(resid1_v, resid_out.at[1], out_sem.at[1]))
+    copies[1].start()
     proj1 = project(resid1, column(mass[...], 1))
-    coef_out[...] = coef_half[...] - RATE * grad(wt_high[...], wt_low[...], proj1)
+    for m in range(2):
+        at = pl.ds(m * 256, 256)
+        coef_v[at, :] = coef_half[at, :] - RATE * grad(wt_high[at, :], wt_low[at, :], proj1)
+        copies.append(pltpu.make_async_copy(coef_v.at[at], coef_out.at[at], out_sem.at[2 + m]))
+        copies[2 + m].start()
+    for copy in copies:
+        copy.wait()
 
 
 def body(table, target_table, centres, coefficients, batch_index):
@@ -324,7 +355,7 @@
             pltpu.VMEM((512, 256), BF16),
             pltpu.VMEM((ND, 16, 128), BF16),
             pltpu.VMEM((ND, 16, 128), BF16),
-            pltpu.VMEM((NZ, NY, 16, 1024), BF16),
+            pltpu.VMEM((NZ, 8, NY, 16, 128), BF16),
             pltpu.VMEM((512, 512), BF16),
             pltpu.VMEM((512, 512), BF16),
             pltpu.VMEM((512, 256), BF16),
@@ -333,7 +364,7 @@
             *[pltpu.VMEM((NZ, n, 128), F32) for n in SHARE],
             pltpu.VMEM((2, NP, 16, 128), F32),
             pltpu.VMEM((2, NP, 16, 128), F32),
-            dma((5,)), dma((4,)), dma, dma((NZ,)), dma((3,)), dma((3,)),
+            dma((5,)), dma((5,)), dma, dma((NZ,)), dma((4,)), dma((6,)),
             dma((15,)), dma((3,)), dma((3,)), dma((3,)), dma((3,)), dma((3,)),
         ],
         compiler_params=pltpu.CompilerParams(
@@ -351,7 +382,8 @@
             jax.ShapeDtypeStruct((2, 256, 256), F32),
         ),
         in_specs=[vmem] * 7,
-        out_specs=(vmem, vmem),
+        out_specs=(pl.BlockSpec(memory_space=pl.ANY), pl.BlockSpec(memory_space=pl.ANY)),
+        scratch_shapes=[pltpu.VMEM((512, 256), F32), pltpu.VMEM((256, 256), F32), dma((4,))],
         compiler_params=pltpu.CompilerParams(vmem_limit_bytes=24 * 2**20),
     )(*sums)
 

time: 54.2 us -> 53.2 us (0.982)
  Pallas kernels: 53.5 us -> 52.5 us
    pallas_call x1, Pallas kernels: 52.1 us -> 51.2 us  [body(): pl.pallas_call(exchange, name='exchange', out_shape=(jax.ShapeDtypeStruct...]
where the time goes in v5:
time: 53.2 us; the launch traced here: 53.1 us
  Pallas kernels  52.5 us (99%)
  between operations  0.64 us (1%)
    pallas_call x1, Pallas kernels, body(): pl.pallas_call(exchange, name='exchange', out_shape=(jax.ShapeDtypeStruct...  51.2 us
    pallas_call x1, Pallas kernels, body(): pl.pallas_call(update, name='update', out_shape=(jax.ShapeDtypeStruct((51...  1.34 us

profile of v5, /device:TPU:1, one launch (start us, length us, event | category | flops | bytes accessed | tf_op | source)
XLA Modules:
  0.0 53.1 jit_solution(7793366612641878139)
XLA Ops:
  0.6 51.2 %exchange.1 = (f32[2,16,16,128]{3,2,1,0:T(8,128)S(1)}, f32[256,256]{1,0:T(8,128)S(1)}, f32[8,128]{1,0:T(8,128)S(1)}, bf16[512,256]{1,0:T(8,128)(2,1)S(1)}, bf16[...) custom-call(bf16[512,1024]{1,0:T(8,128)(2,1)} %table.1, bf16[512,256]{1,0:T(8,128)(2,1)} %target.1, ...), custom_call_target="tpu_custom_call" | custom-call | tf_op jit(solution)/shard_map/exchange/pallas_call | solution.py:333
  51.8 1.3 %update.1 = (f32[512,256]{1,0:T(8,128)}, f32[2,256,256]{2,1,0:T(8,128)}) custom-call(f32[2,16,16,128]{3,2,1,0:T(8,128)S(1)} %get-tuple-element.9.whole2, f32[256,256]{1,0:T(8,128)S(1)} %get-tuple-element.10.turn, f32[8,128]{1,0:T(8,128)S(1)} %get-tuple-element.11.mass, bf16[512,256]{1,0:T(8,128)(2,1)S(1)} %get-tuple-element.12.wt_high, ...), custom_call_target="tpu_custom_call" | custom-call | tf_op jit(solution)/shard_map/update/pallas_call | solution.py:377

commit v6 on v5

--- a/solution.py
+++ b/solution.py
@@ -47,8 +47,8 @@
 
 
 SLOTS = [0, 2, 6, 3, 5, 4, 1, 7]
-GROUPS = [(0, 1), (1, 2), (2, 3), (3, 6)]
-SHARE = (16, 24, 16)
+GROUPS = [(0, 1), (1, 2), (2, 3), (3, 5), (5, 6)]
+SHARE = (16, 16, 24)
 
 
 def pieces_to_whole(whole):
@@ -80,13 +80,13 @@
     whole2, turn_out, mass_out, wt_high, wt_low, coef_half, resid0_out,
     tab_v, tgt_v, cen_v, cf_v, idx_v, aims_v, cf_high, cf_low,
     pick, parts, rows, w_high, w_low, wt0_high, wt0_low,
-    core_send0, core_send1, core_send2, core_recv0, core_recv1, core_recv2,
+    terms0, terms1, terms2, core_recv0, core_recv1, core_recv2,
     xy_send0, xy_send1, xy_send2, xy_recv0, xy_recv1, xy_recv2,
     z_buf0, z_buf1, z_buf2, whole0, whole1,
     load_sem, a_sent, a_recv, az_recv, axy_recv, ac_recv,
     c_sent, cc_recv, cxy_recv, cz_recv, gxy_recv, gc_recv,
 ):
-    core_send, core_recv = (core_send0, core_send1, core_send2), (core_recv0, core_recv1, core_recv2)
+    terms, core_recv = (terms0, terms1, terms2), (core_recv0, core_recv1, core_recv2)
     xy_send, xy_recv = (xy_send0, xy_send1, xy_send2), (xy_recv0, xy_recv1, xy_recv2)
     z_buf, whole = (z_buf0, z_buf1, z_buf2), (whole0, whole1, whole2)
     g = lax.axis_index("grp")
@@ -203,10 +203,16 @@
         wait_group(n)
     for slot in (6, 7):
         wait_bytes(rows.at[0, pl.ds(0, NX)], az_recv.at[SLOTS[slot]])
-        to_sibling(slot, slot + 1, slot - 2)
+        to_sibling(slot, slot + 1, slot - 1)
     wait_group(3)
-
-    for b, e, arrivals in ((0, 3, ((0, 1), (1, 1), (2, 1))), (6, 8, ((4, 1), (5, 1))), (3, 6, ((3, 3),))):
+    wait_group(4)
+
+    for b, e, arrivals in (
+        (0, 3, ((0, 1), (1, 1), (2, 1))),
+        (6, 8, ((5, 1), (6, 1))),
+        (3, 5, ((3, 2),)),
+        (5, 6, ((4, 1),)),
+    ):
         for n, blocks in arrivals:
             wait_bytes(rows.at[pl.ds(0, blocks), pl.ds(0, NX)], ac_recv.at[n])
         some = jnp.concatenate([rows[b:e, f].reshape((e - b) * 64, 128) for f in range(8)], axis=1)
@@ -219,9 +225,8 @@
             w_high[at, :] = high[(r - b) * 64 : (r - b) * 64 + 64]
             w_low[at, :] = low[(r - b) * 64 : (r - b) * 64 + 64]
 
-    def terms(n, h, dst):
-        s = n // 2
-        at = pl.ds(pl.multiple_of(h * 128 + (0, 256, 256)[n], 128), 128)
+    for n in range(3):
+        at = pl.ds(256 if n else 0, 256)
         high, low = w_high[at, :], w_low[at, :]
         if n == 1:
             gh, gl = w_high[0:256, :], w_low[0:256, :]
@@ -229,26 +234,22 @@
         else:
             ch, cl = cf_high[...], cf_low[...]
             part = dot(high, ch) + (dot(high, cl) + dot(low, ch)) - aims_v[at, :]
-        for m in range(2):
-            dst[:, m * 8 : m * 8 + 8, :] = part[:, m * 128 : m * 128 + 128].reshape(NP, 8, 128)
-
-    for n in range(3):
-        terms(n, 1 - c, core_send[n])
-        if n == 1:
+        for h in range(2):
+            for m in range(2):
+                tiles = part[h * 128 : h * 128 + 128, m * 128 : m * 128 + 128].reshape(NP, 8, 128)
+                terms[n][h, :, m * 8 : m * 8 + 8, :] = tiles
+        if n == 2:
             ones = jnp.ones((8, 512), BF16)
             mass = dot(ones, w_high[...], NT) + dot(ones, w_low[...], NT)
             mass = jnp.concatenate(
                 [mass[0:1, m * 128 : m * 128 + 128] for m in range(4)] + [jnp.zeros((4, 128), F32)],
                 axis=0,
             )
-            mass = jnp.broadcast_to(mass[None], (NP, 8, 128))
-            core_send[1][:, 16:24, :] = mass
-            xy_send[1][:, 16:24, :] = mass
-        send(core_send[n], core_recv[n], c_sent.at[n], cc_recv.at[n], sibling)
-    for n in range(3):
-        terms(n, c, xy_send[n])
+            terms[2][:, :, 16:24, :] = jnp.broadcast_to(mass[None, None], (2, NP, 8, 128))
+        send(terms[n].at[1 - c], core_recv[n], c_sent.at[n], cc_recv.at[n], sibling)
+    for n in range(3):
         wait_bytes(core_recv[n], cc_recv.at[n])
-        xy_send[n][...] = xy_send[n][...] + core_recv[n][...]
+        xy_send[n][...] = terms[n][c] + core_recv[n][...]
         for o in XY_FAR:
             send(
                 xy_send[n].at[xs[o[0]] * NY + ys[o[1]]], xy_recv[n].at[p],
@@ -272,14 +273,14 @@
         whole[n][c, p] = total[0:16]
         for o in XY_FAR:
             send(whole[n].at[c, p], whole[n].at[c, p], c_sent.at[9 + n], gxy_recv.at[n], at_xy(o))
-        if n == 1:
+        if n == 2:
             mass = total[16:24]
-            mass_out[...] = mass
-            m0 = column(mass, 0)
     def whole_to_sibling(n):
         wait_bytes(whole[n].at[0, pl.ds(0, NP - 1)], gxy_recv.at[n])
         send(whole[n].at[c], whole[n].at[c], c_sent.at[12 + n], gc_recv.at[n], sibling)
 
+    m0 = column(mass, 0)
+    mass_out[...] = column(mass, 1)
     whole_to_sibling(0)
     whole_to_sibling(1)
     wait_bytes(whole[0].at[0], gc_recv.at[0])
@@ -314,7 +315,7 @@
     resid1_v[...] = resid1
     copies.append(pltpu.make_async_copy(resid1_v, resid_out.at[1], out_sem.at[1]))
     copies[1].start()
-    proj1 = project(resid1, column(mass[...], 1))
+    proj1 = project(resid1, mass[...])
     for m in range(2):
         at = pl.ds(m * 256, 256)
         coef_v[at, :] = coef_half[at, :] - RATE * grad(wt_high[at, :], wt_low[at, :], proj1)
@@ -336,7 +337,7 @@
         out_shape=(
             jax.ShapeDtypeStruct((2, NP, 16, 128), F32),
             square,
-            jax.ShapeDtypeStruct((8, 128), F32),
+            square,
             turned,
             turned,
             jax.ShapeDtypeStruct((512, 256), F32),
@@ -360,11 +361,12 @@
             pltpu.VMEM((512, 512), BF16),
             pltpu.VMEM((512, 256), BF16),
             pltpu.VMEM((512, 256), BF16),
-            *per_peer, *per_peer, *per_peer, *per_peer,
+            *[pltpu.VMEM((2, NP, n, 128), F32) for n in SHARE],
+            *per_peer, *per_peer, *per_peer,
             *[pltpu.VMEM((NZ, n, 128), F32) for n in SHARE],
             pltpu.VMEM((2, NP, 16, 128), F32),
             pltpu.VMEM((2, NP, 16, 128), F32),
-            dma((5,)), dma((5,)), dma, dma((NZ,)), dma((4,)), dma((6,)),
+            dma((5,)), dma((5,)), dma, dma((NZ,)), dma((5,)), dma((7,)),
             dma((15,)), dma((3,)), dma((3,)), dma((3,)), dma((3,)), dma((3,)),
         ],
         compiler_params=pltpu.CompilerParams(

time: 53.2 us -> 53.7 us (level)
  no operation moved by 1% of the time
where the time goes in v6:
time: 53.7 us; the launch traced here: 53.6 us
  Pallas kernels  53 us (99%)
  between operations  0.64 us (1%)
    pallas_call x1, Pallas kernels, body(): pl.pallas_call(exchange, name='exchange', out_shape=(jax.ShapeDtypeStruct...  51.7 us
    pallas_call x1, Pallas kernels, body(): pl.pallas_call(update, name='update', out_shape=(jax.ShapeDtypeStruct((51...  1.3 us

profile of v6, /device:TPU:1, one launch (start us, length us, event | category | flops | bytes accessed | tf_op | source)
XLA Modules:
  0.0 53.6 jit_solution(5472686418814790715)
XLA Ops:
  0.6 51.7 %exchange.1 = (f32[2,16,16,128]{3,2,1,0:T(8,128)S(1)}, f32[256,256]{1,0:T(8,128)S(1)}, f32[256,256]{1,0:T(8,128)S(1)}, bf16[512,256]{1,0:T(8,128)(2,1)S(1)}, bf1...) custom-call(bf16[512,1024]{1,0:T(8,128)(2,1)} %table.1, bf16[512,256]{1,0:T(8,128)(2,1)} %target.1, ...), custom_call_target="tpu_custom_call" | custom-call | tf_op jit(solution)/shard_map/exchange/pallas_call | solution.py:334
  52.3 1.3 %update.1 = (f32[512,256]{1,0:T(8,128)}, f32[2,256,256]{2,1,0:T(8,128)}) custom-call(f32[2,16,16,128]{3,2,1,0:T(8,128)S(1)} %get-tuple-element.9.whole2, f32[256,256]{1,0:T(8,128)S(1)} %get-tuple-element.10.turn, f32[256,256]{1,0:T(8,128)S(1)} %get-tuple-element.11.mass, bf16[512,256]{1,0:T(8,128)(2,1)S(1)} %get-tuple-element.12.wt_high, ...), custom_call_target="tpu_custom_call" | custom-call | tf_op jit(solution)/shard_map/update/pallas_call | solution.py:379

commit v7 on v6

--- a/solution.py
+++ b/solution.py
@@ -47,7 +47,7 @@
 
 
 SLOTS = [0, 2, 6, 3, 5, 4, 1, 7]
-GROUPS = [(0, 1), (1, 2), (2, 3), (3, 5), (5, 6)]
+GROUPS = [(0, 1), (1, 2), (2, 3), (3, 6)]
 SHARE = (16, 16, 24)
 
 
@@ -203,15 +203,13 @@
         wait_group(n)
     for slot in (6, 7):
         wait_bytes(rows.at[0, pl.ds(0, NX)], az_recv.at[SLOTS[slot]])
-        to_sibling(slot, slot + 1, slot - 1)
+        to_sibling(slot, slot + 1, slot - 2)
     wait_group(3)
-    wait_group(4)
 
     for b, e, arrivals in (
         (0, 3, ((0, 1), (1, 1), (2, 1))),
-        (6, 8, ((5, 1), (6, 1))),
-        (3, 5, ((3, 2),)),
-        (5, 6, ((4, 1),)),
+        (6, 8, ((4, 1), (5, 1))),
+        (3, 6, ((3, 3),)),
     ):
         for n, blocks in arrivals:
             wait_bytes(rows.at[pl.ds(0, blocks), pl.ds(0, NX)], ac_recv.at[n])
@@ -366,7 +364,7 @@
             *[pltpu.VMEM((NZ, n, 128), F32) for n in SHARE],
             pltpu.VMEM((2, NP, 16, 128), F32),
             pltpu.VMEM((2, NP, 16, 128), F32),
-            dma((5,)), dma((5,)), dma, dma((NZ,)), dma((5,)), dma((7,)),
+            dma((5,)), dma((5,)), dma, dma((NZ,)), dma((4,)), dma((6,)),
             dma((15,)), dma((3,)), dma((3,)), dma((3,)), dma((3,)), dma((3,)),
         ],
         compiler_params=pltpu.CompilerParams(

time: 53.7 us -> 53 us (0.987)
  Pallas kernels: 53 us -> 52.3 us
    pallas_call x1, Pallas kernels: 51.7 us -> 51 us  [body(): pl.pallas_call(exchange, name='exchange', out_shape=(jax.ShapeDtypeStruct...]
where the time goes in v7:
time: 53 us; the launch traced here: 52.9 us
  Pallas kernels  52.3 us (99%)
  between operations  0.64 us (1%)
    pallas_call x1, Pallas kernels, body(): pl.pallas_call(exchange, name='exchange', out_shape=(jax.ShapeDtypeStruct...  51 us
    pallas_call x1, Pallas kernels, body(): pl.pallas_call(update, name='update', out_shape=(jax.ShapeDtypeStruct((51...  1.3 us

profile of v7, /device:TPU:1, one launch (start us, length us, event | category | flops | bytes accessed | tf_op | source)
XLA Modules:
  0.0 52.9 jit_solution(6275333956201070599)
XLA Ops:
  0.6 51.0 %exchange.1 = (f32[2,16,16,128]{3,2,1,0:T(8,128)S(1)}, f32[256,256]{1,0:T(8,128)S(1)}, f32[256,256]{1,0:T(8,128)S(1)}, bf16[512,256]{1,0:T(8,128)(2,1)S(1)}, bf1...) custom-call(bf16[512,1024]{1,0:T(8,128)(2,1)} %table.1, bf16[512,256]{1,0:T(8,128)(2,1)} %target.1, ...), custom_call_target="tpu_custom_call" | custom-call | tf_op jit(solution)/shard_map/exchange/pallas_call | solution.py:332
  51.6 1.3 %update.1 = (f32[512,256]{1,0:T(8,128)}, f32[2,256,256]{2,1,0:T(8,128)}) custom-call(f32[2,16,16,128]{3,2,1,0:T(8,128)S(1)} %get-tuple-element.9.whole2, f32[256,256]{1,0:T(8,128)S(1)} %get-tuple-element.10.turn, f32[256,256]{1,0:T(8,128)S(1)} %get-tuple-element.11.mass, bf16[512,256]{1,0:T(8,128)(2,1)S(1)} %get-tuple-element.12.wt_high, ...), custom_call_target="tpu_custom_call" | custom-call | tf_op jit(solution)/shard_map/update/pallas_call | solution.py:377

commit v8 on v7

v8 whole, which is shorter than its diff:
```python
import math

import jax
import jax.numpy as jnp
from jax import lax
from jax.experimental import pallas as pl
from jax.experimental.pallas import tpu as pltpu
from jax.sharding import PartitionSpec as P

MESH = pl.DeviceIdType.MESH
SPREAD = 2.0
RATE = 2.0
NX, NC, NY, NZ = 4, 2, 4, 8
NP = NX * NY
ND = NY * NZ
F32 = jnp.float32
BF16 = jnp.bfloat16
HI = lax.Precision.HIGHEST
NN = (((1,), (0,)), ((), ()))
NT = (((1,), (1,)), ((), ()))
TN = (((0,), (0,)), ((), ()))


def hops(k, n):
    return min(k, n - k)


Z_FAR = sorted(range(1, NZ), key=lambda k: -hops(k, NZ))
Z_NEAR = Z_FAR[::-1]
XY_FAR = sorted(
    [(i, j) for i in range(NX) for j in range(NY) if i or j],
    key=lambda o: -hops(o[0], NX) - hops(o[1], NY),
)
YZ_FAR = sorted(
    [(j, k) for j in range(NY) for k in range(NZ) if j or k],
    key=lambda o: -hops(o[0], NY) - hops(o[1], NZ),
)


def dot(a, b, dims=NN, precision=None):
    return lax.dot_general(a, b, dims, precision=precision, preferred_element_type=F32)


def split(a):
    high = a.astype(BF16)
    return high, (a - high.astype(F32)).astype(BF16)


SLOTS = [0, 2, 6, 3, 5, 4, 1, 7]
GROUPS = [(0, 1), (1, 2), (2, 3), (3, 6)]
SHARE = (16, 16, 24)


def pieces_to_whole(whole):
    halves = [
        jnp.concatenate([whole[h, :, m * 8 : m * 8 + 8, :].reshape(128, 128) for m in range(2)], axis=1)
        for h in range(2)
    ]
    return jnp.concatenate(halves, axis=0)


def column(mass, s):
    tiles = [jnp.broadcast_to(mass[h, s : s + 1, :], (128, 128)).T for h in range(2)]
    tall = jnp.concatenate(tiles, axis=0)
    return jnp.concatenate([tall, tall], axis=1)


def project(resid, m):
    along = jnp.sum(m * resid, axis=0, keepdims=True) / jnp.sum(m * m, axis=0, keepdims=True)
    return resid - m * along


def grad(high, low, proj):
    ph, pw = split(proj)
    return dot(high, ph) + (dot(high, pw) + dot(low, ph))


def exchange(
    table, target, centres, coef, index,
    resid1_out, mass_out, wt_high, wt_low, coef_half, resid0_out,
    tab_v, tgt_v, cen_v, cnorm_v, cf_v, idx_v, aims_v, cf_high, cf_low,
    pick, parts, rows, w_high, w_low, w0_high, w0_low, w0_other_high, w0_other_low, w1_high, w1_low,
    wt0_high, wt0_low, mass_all,
    xy_send0, xy_send1, xy_send2, xy_recv0, xy_recv1, xy_recv2,
    z_buf0, z_buf1, z_buf2, whole0, whole1, whole2,
    load_sem, a_sent, a_recv, az_recv, axy_recv, pair_sent, pair_recv,
    c_sent, cxy_recv, cz_recv, gxy_recv, gc_recv,
):
    xy_send, xy_recv = (xy_send0, xy_send1, xy_send2), (xy_recv0, xy_recv1, xy_recv2)
    z_buf, whole = (z_buf0, z_buf1, z_buf2), (whole0, whole1, whole2)
    g = lax.axis_index("grp")
    d = lax.axis_index("dev")
    x, c = g // 2, g % 2
    y, z = d // NZ, d % NZ
    p = x * NY + y
    chunk = z * NY + y
    radius = math.sqrt(2.0 * 1024)
    scale = 1.0 / math.sqrt(131072)

    xs = [lax.rem(x + k, NX) for k in range(NX)]
    ys = [lax.rem(y + k, NY) for k in range(NY)]
    zs = [lax.rem(z + k, NZ) for k in range(NZ)]
    grps = [v * 2 + c for v in xs]
    bases = [v * NZ for v in ys]

    def at_xy(o):
        return {"grp": grps[o[0]], "dev": bases[o[1]] + z}

    def at_yz(o):
        return {"grp": g, "dev": bases[o[0]] + zs[o[1]]}

    sibling = {"grp": x * 2 + 1 - c, "dev": d}

    def send(src, dst, send_sem, recv_sem, to):
        copy = pltpu.make_async_remote_copy(
            src_ref=src, dst_ref=dst, send_sem=send_sem, recv_sem=recv_sem,
            device_id=to, device_id_type=MESH,
        )
        copy.start()
        return copy

    def wait_bytes(ref, sem):
        pltpu.make_async_copy(ref, ref, sem).wait()

    loads = [
        pltpu.make_async_copy(index, idx_v, load_sem.at[0]),
        pltpu.make_async_copy(
            table.at[:, pl.ds(pl.multiple_of(x * 256, 256), 256)], tab_v, load_sem.at[1]
        ),
        pltpu.make_async_copy(target, tgt_v, load_sem.at[2]),
        pltpu.make_async_copy(centres, cen_v.at[c], load_sem.at[3]),
        pltpu.make_async_copy(coef, cf_v, load_sem.at[4]),
    ]
    for load in loads:
        load.start()

    barrier = pltpu.get_barrier_semaphore()
    greeted = [at_yz(o) for o in YZ_FAR] + [at_xy(o) for o in XY_FAR if o[0]] + [sibling]
    for to in greeted:
        pl.semaphore_signal(barrier, inc=1, device_id=to, device_id_type=MESH)

    loads[0].wait()
    here = lax.broadcasted_iota(jnp.int32, (512, 128), 0) + d * 512
    half = pl.ds(pl.multiple_of(c * 128, 128), 128)
    hot = jnp.concatenate(
        [(here == idx_v[s : s + 1, half]).astype(F32).astype(BF16) for s in range(2)], axis=1
    )
    loads[1].wait()
    mine = dot(hot, tab_v[...], TN).astype(BF16).reshape(NZ, 2, 16, 256)
    for k in range(NY):
        pick[:, k] = mine[:, k // 2, :, k % 2 * 128 : k % 2 * 128 + 128]
    parts[chunk] = pick[z, y]

    pl.semaphore_wait(barrier, len(greeted))

    for o in YZ_FAR:
        send(
            pick.at[zs[o[1]], ys[o[0]]], parts.at[chunk], a_sent.at[0], a_recv, at_yz(o)
        )

    def to_sibling(src, dst, n):
        send(src, dst, pair_sent.at[n], pair_recv.at[n], sibling)

    loads[3].wait()
    to_sibling(cen_v.at[c], cen_v.at[c], 0)
    loads[4].wait()
    cf_high[c], cf_low[c] = split(cf_v[...])
    to_sibling(cf_high.at[c], cf_high.at[c], 1)
    to_sibling(cf_low.at[c], cf_low.at[c], 2)
    high, low = split(jnp.square(cen_v[c].astype(F32)))
    ones = jnp.ones((8, 1024), BF16)
    cnorm_v[c] = dot(ones, high, NT) + dot(ones, low, NT)
    to_sibling(cnorm_v.at[c], cnorm_v.at[c], 3)
    loads[2].wait()
    aims_v[...] = dot(hot, tgt_v[...], TN) * (x == 0).astype(F32)

    wait_bytes(parts.at[pl.ds(0, ND - 1)], a_recv)
    own = jnp.sum(parts[...].astype(F32), axis=0).astype(BF16)
    rows[0, x, y] = own

    mine = rows.at[0, x, y]
    for k in Z_FAR:
        slot = SLOTS.index(NZ - k)
        if slot < 6:
            send(mine, rows.at[slot, x, y], a_sent.at[1], az_recv.at[NZ - k], at_yz((0, k)))
    for n, (b, e) in enumerate(GROUPS):
        for r in SLOTS[b:e]:
            if r:
                wait_bytes(parts.at[0], az_recv.at[r])
        group = rows.at[pl.ds(b, e - b), x, y]
        for o in XY_FAR:
            send(group, group, a_sent.at[2 + n // 3], axy_recv.at[n], at_xy(o))

    def arrived(n):
        if n == 3:
            wait_bytes(xy_recv[2].at[pl.ds(0, NP - 1)], axy_recv.at[n])
        else:
            wait_bytes(parts.at[pl.ds(0, NP - 1)], axy_recv.at[n])

    arrived(0)
    for k, slot in ((1, 7), (7, 6)):
        send(rows.at[0], rows.at[slot], a_sent.at[4], az_recv.at[NZ - k], at_yz((0, k)))
    wait_bytes(cen_v.at[0], pair_recv.at[0])
    wait_bytes(cf_high.at[0], pair_recv.at[1])
    wait_bytes(cf_low.at[0], pair_recv.at[2])
    wait_bytes(cnorm_v.at[0], pair_recv.at[3])
    arrived(1)
    arrived(2)

    def values(b, e):
        n = e - b
        some = jnp.concatenate(
            [
                jnp.concatenate(
                    [rows[b:e, i, 2 * q + f].reshape(n * 16, 128) for i in range(NX) for f in range(2)],
                    axis=1,
                )
                for q in range(2)
            ],
            axis=0,
        )
        rnorm = jnp.sum(jnp.square(some.astype(F32)), axis=1, keepdims=True)
        for k in range(NC):
            cross = dot(some, cen_v[k], NT)
            dist = jnp.sqrt(jnp.maximum(rnorm + cnorm_v[k, 0:1, :] - 2.0 * cross, 0.0))
            high, low = split(jnp.exp((radius - dist) / SPREAD) * scale)
            for q in range(2):
                for r in range(b, e):
                    at = pl.ds(pl.multiple_of(zs[SLOTS[r]] * 32 + q * 16, 16), 16)
                    o = (q * n + r - b) * 16
                    w_high[k, at, :] = high[o : o + 16]
                    w_low[k, at, :] = low[o : o + 16]

    values(0, 3)
    for slot in (6, 7):
        wait_bytes(rows.at[0], az_recv.at[SLOTS[slot]])
    values(6, 8)
    arrived(3)
    values(3, 6)

    first, second = pl.ds(0, 128), pl.ds(128, 128)
    to_sibling(w_high.at[:, first], w0_other_high, 4)
    to_sibling(w_low.at[:, first], w0_other_low, 5)

    def put(part, dst, lane):
        dst[:, lane, :] = part.reshape(NP, 8, 128)

    def share_out(n):
        for o in XY_FAR:
            send(
                xy_send[n].at[xs[o[0]] * NY + ys[o[1]]], xy_recv[n].at[p],
                c_sent.at[n], cxy_recv.at[n], at_xy(o),
            )
        xy_recv[n][p] = xy_send[n][p]

    for s in range(2):
        at = pl.ds(s * 128, 128)
        part = -aims_v[at, :]
        for k in range(NC):
            high, low = w_high[k, at, :], w_low[k, at, :]
            ch, cl = cf_high[k], cf_low[k]
            part = part + (dot(high, ch) + (dot(high, cl) + dot(low, ch)))
        for m in range(2):
            put(part[:, m * 128 : m * 128 + 128], xy_send[s], pl.ds(m * 8, 8))
        share_out(s)
    to_sibling(w_high.at[1 - c, second], w1_high.at[c], 6)
    to_sibling(w_low.at[1 - c, second], w1_low.at[c], 7)

    ones = jnp.ones((8, 512), BF16)
    mass = sum(dot(ones, w_high[k], NT) + dot(ones, w_low[k], NT) for k in range(NC))
    mass = jnp.concatenate([mass[0:1, 0:128], mass[0:1, 128:256], jnp.zeros((6, 128), F32)], axis=0)
    xy_send[2][:, 16:24, :] = jnp.broadcast_to(mass[None], (NP, 8, 128))

    def gram(others):
        part = jnp.zeros((128, 128), F32)
        for k in range(NC):
            high, low = w_high[k, second, :], w_low[k, second, :]
            gh, gl = others(k)
            part = part + (dot(high, gh, NT) + (dot(high, gl, NT) + dot(low, gh, NT)))
        return part

    own_lanes = pl.ds(pl.multiple_of(c * 8, 8), 8)
    other_lanes = pl.ds(pl.multiple_of(8 - c * 8, 8), 8)
    put(gram(lambda k: (w_high[k, first, :], w_low[k, first, :])), xy_send[2], own_lanes)
    wait_bytes(w0_other_high, pair_recv.at[4])
    wait_bytes(w0_other_low, pair_recv.at[5])
    put(gram(lambda k: (w0_other_high[k], w0_other_low[k])), xy_send[2], other_lanes)
    share_out(2)

    w0_high[c], w0_low[c] = w_high[c, first, :], w_low[c, first, :]
    w0_high[1 - c], w0_low[1 - c] = w0_other_high[c], w0_other_low[c]
    wt0_high[...] = w0_high[...].reshape(256, 512).T
    wt0_low[...] = w0_low[...].reshape(256, 512).T
    wait_bytes(w1_high.at[0], pair_recv.at[6])
    wait_bytes(w1_low.at[0], pair_recv.at[7])
    wait_bytes(w1_high.at[0], pair_sent.at[6])
    wait_bytes(w1_low.at[0], pair_sent.at[7])
    w1_high[c], w1_low[c] = w_high[c, second, :], w_low[c, second, :]
    wt_high[...] = w1_high[...].reshape(256, 512).T
    wt_low[...] = w1_low[...].reshape(256, 512).T

    for n in range(3):
        wait_bytes(xy_recv[n].at[pl.ds(0, NP - 1)], cxy_recv.at[n])
        z_buf[n][z] = jnp.sum(xy_recv[n][...], axis=0)
        for k in Z_FAR:
            send(z_buf[n].at[z], z_buf[n].at[z], c_sent.at[3 + n], cz_recv.at[n], at_yz((0, k)))
    for n in range(3):
        wait_bytes(z_buf[n].at[pl.ds(0, NZ - 1)], cz_recv.at[n])
        total = jnp.sum(z_buf[n][...], axis=0)
        whole[n][c, p] = total[0:16]
        for o in XY_FAR:
            send(whole[n].at[c, p], whole[n].at[c, p], c_sent.at[6 + n], gxy_recv.at[n], at_xy(o))
        if n == 2:
            mass_all[c] = total[16:24]
            to_sibling(mass_all.at[c], mass_all.at[c], 8)
    def whole_to_sibling(n):
        wait_bytes(whole[n].at[0, pl.ds(0, NP - 1)], gxy_recv.at[n])
        send(whole[n].at[c], whole[n].at[c], c_sent.at[9 + n], gc_recv.at[n], sibling)

    whole_to_sibling(0)
    wait_bytes(mass_all.at[0], pair_recv.at[8])
    m0 = column(mass_all, 0)
    mass_out[...] = column(mass_all, 1)
    whole_to_sibling(1)
    wait_bytes(whole[0].at[0], gc_recv.at[0])
    resid0 = pieces_to_whole(whole0)
    resid0_out[...] = resid0
    proj0 = project(resid0, m0)
    whole_to_sibling(2)
    coef_half[...] = cf_v[...] - RATE * grad(wt0_high[...], wt0_low[...], proj0)
    wait_bytes(whole[1].at[0], gc_recv.at[1])
    wait_bytes(whole[2].at[0], gc_recv.at[2])
    resid1_out[...] = pieces_to_whole(whole1) - RATE * dot(pieces_to_whole(whole2), proj0, precision=HI)

    wait_bytes(parts.at[pl.ds(0, ND - 1)], a_sent.at[0])
    wait_bytes(parts.at[pl.ds(0, 5)], a_sent.at[1])
    wait_bytes(xy_recv[2].at[pl.ds(0, NP - 1)], a_sent.at[2])
    wait_bytes(xy_recv[2].at[pl.ds(0, NP - 1)], a_sent.at[3])
    wait_bytes(rows.at[pl.ds(0, 2)], a_sent.at[4])
    for n, ref in enumerate((
        cen_v.at[0], cf_high.at[0], cf_low.at[0], cnorm_v.at[0], w0_other_high, w0_other_low, None, None,
        mass_all.at[0],
    )):
        if ref is not None:
            wait_bytes(ref, pair_sent.at[n])
    for n in range(3):
        wait_bytes(xy_recv[n].at[pl.ds(0, NP - 1)], c_sent.at[n])
        wait_bytes(z_buf[n].at[pl.ds(0, NZ - 1)], c_sent.at[3 + n])
        wait_bytes(whole[n].at[0, pl.ds(0, NP - 1)], c_sent.at[6 + n])
        wait_bytes(whole[n].at[0], c_sent.at[9 + n])


def update(
    resid1, mass, wt_high, wt_low, coef_half, resid0, coef_out, resid_out, coef_v, out_sem
):
    copies = [pltpu.make_async_copy(resid0, resid_out.at[0], out_sem.at[0])]
    copies[0].start()
    copies.append(pltpu.make_async_copy(resid1, resid_out.at[1], out_sem.at[1]))
    copies[1].start()
    proj1 = project(resid1[...], mass[...])
    for m in range(2):
        at = pl.ds(m * 256, 256)
        coef_v[at, :] = coef_half[at, :] - RATE * grad(wt_high[at, :], wt_low[at, :], proj1)
        copies.append(pltpu.make_async_copy(coef_v.at[at], coef_out.at[at], out_sem.at[2 + m]))
        copies[2 + m].start()
    for copy in copies:
        copy.wait()


def body(table, target_table, centres, coefficients, batch_index):
    dma = pltpu.SemaphoreType.DMA
    vmem = pl.BlockSpec(memory_space=pltpu.VMEM)
    square = jax.ShapeDtypeStruct((256, 256), F32)
    turned = jax.ShapeDtypeStruct((512, 256), BF16)
    per_peer = [pltpu.VMEM((NP, n, 128), F32) for n in SHARE]
    sums = pl.pallas_call(
        exchange,
        name="exchange",
        out_shape=(
            square,
            square,
            turned,
            turned,
            jax.ShapeDtypeStruct((512, 256), F32),
            square,
        ),
        in_specs=[pl.BlockSpec(memory_space=pl.ANY)] * 5,
        out_specs=(vmem,) * 6,
        scratch_shapes=[
            pltpu.VMEM((512, 256), BF16),
            pltpu.VMEM((512, 256), BF16),
            pltpu.VMEM((NC, 512, 1024), BF16),
            pltpu.VMEM((NC, 8, 512), F32),
            pltpu.VMEM((512, 256), F32),
            pltpu.VMEM((2, 256), jnp.int32),
            pltpu.VMEM((256, 256), F32),
            pltpu.VMEM((NC, 512, 256), BF16),
            pltpu.VMEM((NC, 512, 256), BF16),
            pltpu.VMEM((NZ, NY, 16, 128), BF16),
            pltpu.VMEM((ND, 16, 128), BF16),
            pltpu.VMEM((NZ, NX, NY, 16, 128), BF16),
            *[pltpu.VMEM((NC, 256, 512), BF16) for _ in range(2)],
            *[pltpu.VMEM((NC, 128, 512), BF16) for _ in range(6)],
            *[pltpu.VMEM((512, 256), BF16) for _ in range(2)],
            pltpu.VMEM((NC, 8, 128), F32),
            *per_peer, *per_peer,
            *[pltpu.VMEM((NZ, n, 128), F32) for n in SHARE],
            *[pltpu.VMEM((2, NP, 16, 128), F32) for _ in range(3)],
            dma((5,)), dma((5,)), dma, dma((NZ,)), dma((4,)), dma((9,)), dma((9,)),
            dma((12,)), dma((3,)), dma((3,)), dma((3,)), dma((3,)),
        ],
        compiler_params=pltpu.CompilerParams(
            collective_id=0, has_side_effects=True, vmem_limit_bytes=40 * 2**20
        ),
    )(*[
        pltpu.with_memory_space_constraint(a, pltpu.HBM)
        for a in (table, target_table, centres, coefficients, batch_index)
    ])
    return pl.pallas_call(
        update,
        name="update",
        out_shape=(
            jax.ShapeDtypeStruct((512, 256), F32),
            jax.ShapeDtypeStruct((2, 256, 256), F32),
        ),
        in_specs=[vmem] * 6,
        out_specs=(pl.BlockSpec(memory_space=pl.ANY), pl.BlockSpec(memory_space=pl.ANY)),
        scratch_shapes=[pltpu.VMEM((512, 256), F32), dma((4,))],
        compiler_params=pltpu.CompilerParams(vmem_limit_bytes=24 * 2**20),
    )(*sums)


def solution(mesh):
    in_specs = (
        P("dev", None),
        P("dev", None),
        P(("grp", "dev"), None),
        P(("grp", "dev"), None),
        P(),
    )
    out_specs = (P(("grp", "dev"), None), P())
    return jax.shard_map(body, mesh=mesh, in_specs=in_specs, out_specs=out_specs, check_vma=False)
```

time: 53 us -> 51.6 us (0.974)
  Pallas kernels: 52.3 us -> 50.9 us
    pallas_call x1, Pallas kernels: 51 us -> 49.6 us  [body(): pl.pallas_call(exchange, name='exchange', out_shape=(square, square, turn...]
where the time goes in v8:
time: 51.6 us; the launch traced here: 51.5 us
  Pallas kernels  50.9 us (99%)
  between operations  0.64 us (1%)
    pallas_call x1, Pallas kernels, body(): pl.pallas_call(exchange, name='exchange', out_shape=(square, square, turn...  49.6 us
    pallas_call x1, Pallas kernels, body(): pl.pallas_call(update, name='update', out_shape=(jax.ShapeDtypeStruct((51...  1.27 us

profile of v8, /device:TPU:1, one launch (start us, length us, event | category | flops | bytes accessed | tf_op | source)
XLA Modules:
  0.0 51.5 jit_solution(10072994602179675459)
XLA Ops:
  0.6 49.6 %exchange.1 = (f32[256,256]{1,0:T(8,128)S(1)}, f32[256,256]{1,0:T(8,128)S(1)}, bf16[512,256]{1,0:T(8,128)(2,1)S(1)}, bf16[512,256]{1,0:T(8,128)(2,1)S(1)}, f32[5...) custom-call(bf16[512,1024]{1,0:T(8,128)(2,1)} %table.1, bf16[512,256]{1,0:T(8,128)(2,1)} %target.1, bf16[512,1024]{1,0:T(8,128)(2,1)} %centres.1, ...), custom_call_target="tpu_custom_call" | custom-call | tf_op jit(solution)/shard_map/exchange/pallas_call | solution.py:376
  50.2 1.3 %update.1 = (f32[512,256]{1,0:T(8,128)}, f32[2,256,256]{2,1,0:T(8,128)}) custom-call(f32[256,256]{1,0:T(8,128)S(1)} %get-tuple-element.8.resid1, f32[256,256]{1,0:T(8,128)S(1)} %get-tuple-element.9.mass, bf16[512,256]{1,0:T(8,128)(2,1)S(1)} %get-tuple-element.10.wt_high, bf16[512,256]{1,0:T(8,128)(2,1)S(1)} %get-tuple-element.11.wt_low, ...), custom_call_target="tpu_custom_call" | custom-call | tf_op jit(solution)/shard_map/update/pallas_call | solution.py:419

commit v9 on v8

--- a/solution.py
+++ b/solution.py
@@ -51,12 +51,12 @@
 SHARE = (16, 16, 24)
 
 
+def rows_of(whole, h):
+    return jnp.concatenate([whole[h, :, m * 8 : m * 8 + 8, :].reshape(128, 128) for m in range(2)], axis=1)
+
+
 def pieces_to_whole(whole):
-    halves = [
-        jnp.concatenate([whole[h, :, m * 8 : m * 8 + 8, :].reshape(128, 128) for m in range(2)], axis=1)
-        for h in range(2)
-    ]
-    return jnp.concatenate(halves, axis=0)
+    return jnp.concatenate([rows_of(whole, h) for h in range(2)], axis=0)
 
 
 def column(mass, s):
@@ -313,24 +313,22 @@
         if n == 2:
             mass_all[c] = total[16:24]
             to_sibling(mass_all.at[c], mass_all.at[c], 8)
-    def whole_to_sibling(n):
-        wait_bytes(whole[n].at[0, pl.ds(0, NP - 1)], gxy_recv.at[n])
-        send(whole[n].at[c], whole[n].at[c], c_sent.at[9 + n], gc_recv.at[n], sibling)
-
-    whole_to_sibling(0)
+    wait_bytes(whole[0].at[0, pl.ds(0, NP - 1)], gxy_recv.at[0])
+    send(whole[0].at[c], whole[0].at[c], c_sent.at[9], gc_recv.at[0], sibling)
     wait_bytes(mass_all.at[0], pair_recv.at[8])
     m0 = column(mass_all, 0)
     mass_out[...] = column(mass_all, 1)
-    whole_to_sibling(1)
     wait_bytes(whole[0].at[0], gc_recv.at[0])
     resid0 = pieces_to_whole(whole0)
     resid0_out[...] = resid0
     proj0 = project(resid0, m0)
-    whole_to_sibling(2)
+    wait_bytes(whole[1].at[0, pl.ds(0, NP - 1)], gxy_recv.at[1])
+    wait_bytes(whole[2].at[0, pl.ds(0, NP - 1)], gxy_recv.at[2])
+    own_rows = pl.ds(pl.multiple_of(c * 128, 128), 128)
+    resid1_out[own_rows, :] = rows_of(whole1, c) - RATE * dot(rows_of(whole2, c), proj0, precision=HI)
+    send(resid1_out.at[own_rows], resid1_out.at[own_rows], c_sent.at[10], gc_recv.at[1], sibling)
     coef_half[...] = cf_v[...] - RATE * grad(wt0_high[...], wt0_low[...], proj0)
-    wait_bytes(whole[1].at[0], gc_recv.at[1])
-    wait_bytes(whole[2].at[0], gc_recv.at[2])
-    resid1_out[...] = pieces_to_whole(whole1) - RATE * dot(pieces_to_whole(whole2), proj0, precision=HI)
+    wait_bytes(resid1_out.at[pl.ds(0, 128)], gc_recv.at[1])
 
     wait_bytes(parts.at[pl.ds(0, ND - 1)], a_sent.at[0])
     wait_bytes(parts.at[pl.ds(0, 5)], a_sent.at[1])
@@ -347,7 +345,8 @@
         wait_bytes(xy_recv[n].at[pl.ds(0, NP - 1)], c_sent.at[n])
         wait_bytes(z_buf[n].at[pl.ds(0, NZ - 1)], c_sent.at[3 + n])
         wait_bytes(whole[n].at[0, pl.ds(0, NP - 1)], c_sent.at[6 + n])
-        wait_bytes(whole[n].at[0], c_sent.at[9 + n])
+    wait_bytes(whole[0].at[0], c_sent.at[9])
+    wait_bytes(resid1_out.at[pl.ds(0, 128)], c_sent.at[10])
 
 
 def update(
@@ -407,7 +406,7 @@
             *[pltpu.VMEM((NZ, n, 128), F32) for n in SHARE],
             *[pltpu.VMEM((2, NP, 16, 128), F32) for _ in range(3)],
             dma((5,)), dma((5,)), dma, dma((NZ,)), dma((4,)), dma((9,)), dma((9,)),
-            dma((12,)), dma((3,)), dma((3,)), dma((3,)), dma((3,)),
+            dma((11,)), dma((3,)), dma((3,)), dma((3,)), dma((2,)),
         ],
         compiler_params=pltpu.CompilerParams(
             collective_id=0, has_side_effects=True, vmem_limit_bytes=40 * 2**20

time: 51.6 us -> 51.2 us (level)
  no operation moved by 1% of the time
where the time goes in v9:
time: 51.2 us; the launch traced here: 51.1 us
  Pallas kernels  50.5 us (99%)
  between operations  0.64 us (1%)
    pallas_call x1, Pallas kernels, body(): pl.pallas_call(exchange, name='exchange', out_shape=(square, square, turn...  49.2 us
    pallas_call x1, Pallas kernels, body(): pl.pallas_call(update, name='update', out_shape=(jax.ShapeDtypeStruct((51...  1.27 us

profile of v9, /device:TPU:1, one launch (start us, length us, event | category | flops | bytes accessed | tf_op | source)
XLA Modules:
  0.0 51.1 jit_solution(13582069510240900907)
XLA Ops:
  0.6 49.2 %exchange.1 = (f32[256,256]{1,0:T(8,128)S(1)}, f32[256,256]{1,0:T(8,128)S(1)}, bf16[512,256]{1,0:T(8,128)(2,1)S(1)}, bf16[512,256]{1,0:T(8,128)(2,1)S(1)}, f32[5...) custom-call(bf16[512,1024]{1,0:T(8,128)(2,1)} %table.1, bf16[512,256]{1,0:T(8,128)(2,1)} %target.1, bf16[512,1024]{1,0:T(8,128)(2,1)} %centres.1, ...), custom_call_target="tpu_custom_call" | custom-call | tf_op jit(solution)/shard_map/exchange/pallas_call | solution.py:375
  49.8 1.3 %update.1 = (f32[512,256]{1,0:T(8,128)}, f32[2,256,256]{2,1,0:T(8,128)}) custom-call(f32[256,256]{1,0:T(8,128)S(1)} %get-tuple-element.8.resid1, f32[256,256]{1,0:T(8,128)S(1)} %get-tuple-element.9.mass, bf16[512,256]{1,0:T(8,128)(2,1)S(1)} %get-tuple-element.10.wt_high, bf16[512,256]{1,0:T(8,128)(2,1)S(1)} %get-tuple-element.11.wt_low, ...), custom_call_target="tpu_custom_call" | custom-call | tf_op jit(solution)/shard_map/update/pallas_call | solution.py:418

commit v10 on v9

--- a/solution.py
+++ b/solution.py
@@ -253,16 +253,14 @@
             )
         xy_recv[n][p] = xy_send[n][p]
 
-    for s in range(2):
-        at = pl.ds(s * 128, 128)
-        part = -aims_v[at, :]
-        for k in range(NC):
-            high, low = w_high[k, at, :], w_low[k, at, :]
-            ch, cl = cf_high[k], cf_low[k]
-            part = part + (dot(high, ch) + (dot(high, cl) + dot(low, ch)))
+    part = -aims_v[...]
+    for k in range(NC):
+        high, low, ch, cl = w_high[k], w_low[k], cf_high[k], cf_low[k]
+        part = part + (dot(high, ch) + (dot(high, cl) + dot(low, ch)))
+    for n in range(2):
         for m in range(2):
-            put(part[:, m * 128 : m * 128 + 128], xy_send[s], pl.ds(m * 8, 8))
-        share_out(s)
+            put(part[n * 128 : n * 128 + 128, m * 128 : m * 128 + 128], xy_send[n], pl.ds(m * 8, 8))
+        share_out(n)
     to_sibling(w_high.at[1 - c, second], w1_high.at[c], 6)
     to_sibling(w_low.at[1 - c, second], w1_low.at[c], 7)
 

time: 51.2 us -> 51.8 us (1.012)
  Pallas kernels: 50.5 us -> 51.1 us
    pallas_call x1, Pallas kernels: 49.2 us -> 49.8 us  [body(): pl.pallas_call(exchange, name='exchange', out_shape=(square, square, turn...]
where the time goes in v10:
time: 51.8 us; the launch traced here: 51.7 us
  Pallas kernels  51.1 us (99%)
  between operations  0.64 us (1%)
    pallas_call x1, Pallas kernels, body(): pl.pallas_call(exchange, name='exchange', out_shape=(square, square, turn...  49.8 us
    pallas_call x1, Pallas kernels, body(): pl.pallas_call(update, name='update', out_shape=(jax.ShapeDtypeStruct((51...  1.27 us

profile of v10, /device:TPU:1, one launch (start us, length us, event | category | flops | bytes accessed | tf_op | source)
XLA Modules:
  0.0 51.7 jit_solution(17435782111927728649)
XLA Ops:
  0.6 49.8 %exchange.1 = (f32[256,256]{1,0:T(8,128)S(1)}, f32[256,256]{1,0:T(8,128)S(1)}, bf16[512,256]{1,0:T(8,128)(2,1)S(1)}, bf16[512,256]{1,0:T(8,128)(2,1)S(1)}, f32[5...) custom-call(bf16[512,1024]{1,0:T(8,128)(2,1)} %table.1, bf16[512,256]{1,0:T(8,128)(2,1)} %target.1, bf16[512,1024]{1,0:T(8,128)(2,1)} %centres.1, ...), custom_call_target="tpu_custom_call" | custom-call | tf_op jit(solution)/shard_map/exchange/pallas_call | solution.py:373
  50.4 1.3 %update.1 = (f32[512,256]{1,0:T(8,128)}, f32[2,256,256]{2,1,0:T(8,128)}) custom-call(f32[256,256]{1,0:T(8,128)S(1)} %get-tuple-element.8.resid1, f32[256,256]{1,0:T(8,128)S(1)} %get-tuple-element.9.mass, bf16[512,256]{1,0:T(8,128)(2,1)S(1)} %get-tuple-element.10.wt_high, bf16[512,256]{1,0:T(8,128)(2,1)S(1)} %get-tuple-element.11.wt_low, ...), custom_call_target="tpu_custom_call" | custom-call | tf_op jit(solution)/shard_map/update/pallas_call | solution.py:416

commit v11 on v9

--- a/solution.py
+++ b/solution.py
@@ -122,6 +122,11 @@
     def wait_bytes(ref, sem):
         pltpu.make_async_copy(ref, ref, sem).wait()
 
+    barrier = pltpu.get_barrier_semaphore()
+    greeted = [at_yz(o) for o in YZ_FAR] + [at_xy(o) for o in XY_FAR if o[0]] + [sibling]
+    for to in greeted:
+        pl.semaphore_signal(barrier, inc=1, device_id=to, device_id_type=MESH)
+
     loads = [
         pltpu.make_async_copy(index, idx_v, load_sem.at[0]),
         pltpu.make_async_copy(
@@ -133,11 +138,6 @@
     ]
     for load in loads:
         load.start()
-
-    barrier = pltpu.get_barrier_semaphore()
-    greeted = [at_yz(o) for o in YZ_FAR] + [at_xy(o) for o in XY_FAR if o[0]] + [sibling]
-    for to in greeted:
-        pl.semaphore_signal(barrier, inc=1, device_id=to, device_id_type=MESH)
 
     loads[0].wait()
     here = lax.broadcasted_iota(jnp.int32, (512, 128), 0) + d * 512

time: 51.2 us -> 51.2 us (level)
  no operation moved by 1% of the time
where the time goes in v11:
time: 51.2 us; the launch traced here: 51.1 us
  Pallas kernels  50.4 us (98%)
  between operations  0.64 us (1%)
    pallas_call x1, Pallas kernels, body(): pl.pallas_call(exchange, name='exchange', out_shape=(square, square, turn...  49.2 us
    pallas_call x1, Pallas kernels, body(): pl.pallas_call(update, name='update', out_shape=(jax.ShapeDtypeStruct((51...  1.27 us

profile of v11, /device:TPU:1, one launch (start us, length us, event | category | flops | bytes accessed | tf_op | source)
XLA Modules:
  0.0 51.1 jit_solution(5769298316851707527)
XLA Ops:
  0.6 49.2 %exchange.1 = (f32[256,256]{1,0:T(8,128)S(1)}, f32[256,256]{1,0:T(8,128)S(1)}, bf16[512,256]{1,0:T(8,128)(2,1)S(1)}, bf16[512,256]{1,0:T(8,128)(2,1)S(1)}, f32[5...) custom-call(bf16[512,1024]{1,0:T(8,128)(2,1)} %table.1, bf16[512,256]{1,0:T(8,128)(2,1)} %target.1, bf16[512,1024]{1,0:T(8,128)(2,1)} %centres.1, ...), custom_call_target="tpu_custom_call" | custom-call | tf_op jit(solution)/shard_map/exchange/pallas_call | solution.py:375
  49.8 1.3 %update.1 = (f32[512,256]{1,0:T(8,128)}, f32[2,256,256]{2,1,0:T(8,128)}) custom-call(f32[256,256]{1,0:T(8,128)S(1)} %get-tuple-element.8.resid1, f32[256,256]{1,0:T(8,128)S(1)} %get-tuple-element.9.mass, bf16[512,256]{1,0:T(8,128)(2,1)S(1)} %get-tuple-element.10.wt_high, bf16[512,256]{1,0:T(8,128)(2,1)S(1)} %get-tuple-element.11.wt_low, ...), custom_call_target="tpu_custom_call" | custom-call | tf_op jit(solution)/shard_map/update/pallas_call | solution.py:418

commit v12 on v10

--- a/solution.py
+++ b/solution.py
@@ -122,6 +122,11 @@
     def wait_bytes(ref, sem):
         pltpu.make_async_copy(ref, ref, sem).wait()
 
+    barrier = pltpu.get_barrier_semaphore()
+    greeted = [at_yz(o) for o in YZ_FAR] + [at_xy(o) for o in XY_FAR if o[0]] + [sibling]
+    for to in greeted:
+        pl.semaphore_signal(barrier, inc=1, device_id=to, device_id_type=MESH)
+
     loads = [
         pltpu.make_async_copy(index, idx_v, load_sem.at[0]),
         pltpu.make_async_copy(
@@ -133,11 +138,6 @@
     ]
     for load in loads:
         load.start()
-
-    barrier = pltpu.get_barrier_semaphore()
-    greeted = [at_yz(o) for o in YZ_FAR] + [at_xy(o) for o in XY_FAR if o[0]] + [sibling]
-    for to in greeted:
-        pl.semaphore_signal(barrier, inc=1, device_id=to, device_id_type=MESH)
 
     loads[0].wait()
     here = lax.broadcasted_iota(jnp.int32, (512, 128), 0) + d * 512

time: 51.8 us -> 51.7 us (level)
  no operation moved by 1% of the time
where the time goes in v12:
time: 51.7 us; the launch traced here: 51.6 us
  Pallas kernels  50.9 us (98%)
  between operations  0.64 us (1%)
    pallas_call x1, Pallas kernels, body(): pl.pallas_call(exchange, name='exchange', out_shape=(square, square, turn...  49.7 us
    pallas_call x1, Pallas kernels, body(): pl.pallas_call(update, name='update', out_shape=(jax.ShapeDtypeStruct((51...  1.27 us

profile of v12, /device:TPU:1, one launch (start us, length us, event | category | flops | bytes accessed | tf_op | source)
XLA Modules:
  0.0 51.6 jit_solution(17839581013695191373)
XLA Ops:
  0.6 49.7 %exchange.1 = (f32[256,256]{1,0:T(8,128)S(1)}, f32[256,256]{1,0:T(8,128)S(1)}, bf16[512,256]{1,0:T(8,128)(2,1)S(1)}, bf16[512,256]{1,0:T(8,128)(2,1)S(1)}, f32[5...) custom-call(bf16[512,1024]{1,0:T(8,128)(2,1)} %table.1, bf16[512,256]{1,0:T(8,128)(2,1)} %target.1, bf16[512,1024]{1,0:T(8,128)(2,1)} %centres.1, ...), custom_call_target="tpu_custom_call" | custom-call | tf_op jit(solution)/shard_map/exchange/pallas_call | solution.py:373
  50.3 1.3 %update.1 = (f32[512,256]{1,0:T(8,128)}, f32[2,256,256]{2,1,0:T(8,128)}) custom-call(f32[256,256]{1,0:T(8,128)S(1)} %get-tuple-element.8.resid1, f32[256,256]{1,0:T(8,128)S(1)} %get-tuple-element.9.mass, bf16[512,256]{1,0:T(8,128)(2,1)S(1)} %get-tuple-element.10.wt_high, bf16[512,256]{1,0:T(8,128)(2,1)S(1)} %get-tuple-element.11.wt_low, ...), custom_call_target="tpu_custom_call" | custom-call | tf_op jit(solution)/shard_map/update/pallas_call | solution.py:416
